TPU v7x, 32 devices: a whole 2x2x4 slice. The times are simulated.
32 devices in a mesh: blk: 8 (over z, x), head: 4 (over y, core).
Axes of the slice: x: 2, y: 2, z: 4, core: 2. Of those that a mesh axis runs over, the one named last changes fastest.
Arguments:
- inputs: bfloat16 [2, 2048, 1024], P(None, ('blk', 'head')), may hold values from -6 to 6
- cotangent: bfloat16 [2, 2048, 1024], P(None, ('blk', 'head')), may hold values from -6 to 6
- doc_starts: int32 [2, 2], replicated, may hold values from 1 to 2047, as said below
- norm_one: bfloat16 [1024], P(('blk', 'head')), may hold values from 0.5 to 1.5
- mixer_in: bfloat16 [1024, 3352], P(('blk', 'head')), may hold values from -0.1875 to 0.1875
- conv_weight: float32 [4, 1792], replicated, may hold values from -3 to 3
- conv_bias: float32 [1792], replicated, may hold values from -3 to 3
- dt_bias: float32 [24], replicated, may hold values from -7 to -2.25
- a_log: float32 [24], replicated, may hold values from -1 to 1
- d_skip: float32 [24], replicated, may hold values from 0.5 to 1.5
- ssm_gain: float32 [1536], replicated, may hold values from 0.5 to 1.5
- mixer_out: bfloat16 [1536, 1024], P(None, ('blk', 'head')), may hold values from -0.15625 to 0.15625
- attn_in: bfloat16 [1024, 768], P(('blk', 'head')), may hold values from -0.1875 to 0.1875
- attn_out: bfloat16 [512, 1024], P(None, ('blk', 'head')), may hold values from -0.75 to 0.75
- norm_two: bfloat16 [1024], P(('blk', 'head')), may hold values from 0.5 to 1.5
- ffn_in: bfloat16 [1024, 4096], P(('blk', 'head')), may hold values from -0.1875 to 0.1875
- ffn_out: bfloat16 [2048, 1024], P(None, ('blk', 'head')), may hold values from -0.125 to 0.125
Outputs:
- output: float32 [2, 2048, 1024], P(None, ('blk', 'head'))
- grad_inputs: float32 [2, 2048, 1024], P(None, ('blk', 'head'))
- grad_norm_one: float32 [1024], replicated
- grad_mixer_in: float32 [1024, 3352], P('blk', 'head')
- grad_conv_weight: float32 [4, 1792], replicated
- grad_conv_bias: float32 [1792], replicated
- grad_dt_bias: float32 [24], replicated
- grad_a_log: float32 [24], replicated
- grad_d_skip: float32 [24], replicated
- grad_ssm_gain: float32 [1536], replicated
- grad_mixer_out: float32 [1536, 1024], P('blk', 'head')
- grad_attn_in: float32 [1024, 768], P('blk', 'head')
- grad_attn_out: float32 [512, 1024], P('blk', 'head')
- grad_norm_two: float32 [1024], replicated
- grad_ffn_in: float32 [1024, 4096], P('blk', 'head')
- grad_ffn_out: float32 [2048, 1024], P('blk', 'head')
Inputs may be any that keep to these rules, and one draw needn't show every extreme that they name: `doc_starts`: each row is strictly ascending; every document it bounds (from token 0 to the first start, between consecutive starts, from the last start to the end of the 2048 tokens) is at most 1024 tokens long, and one of them is exactly 1024 long.
All inputs are finite; a program needn't handle non-finite values.
Results may differ from a plain program's by a relative error of at most 0.04.
Values may be sent and summed in bfloat16 or wider, within the bound.
A program may use at most 192 MiB of HBM per device.

v0:
```python
import jax
import jax.numpy as jnp
import numpy as np
from jax import lax
from jax.sharding import PartitionSpec as P

MHEADS = 24
MHDIM = 64
STATE = 128
CONVK = 4
QHEADS = 8
KVHEADS = 2
HDIM = 64
FF = 2048
MB = 2
MAXLEN = 4096
DI = 1536


eps_norm = 1e-05
rope_base = 10000.0
far_negative = -1e30
highest = lax.Precision.HIGHEST


def shifted_2(value, axis, steps):
    count = lax.axis_size(axis)
    first, last = (max(0, -steps), min(count, count - steps))
    return lax.ppermute(value, axis, [(source, source + steps) for source in range(first, last)])


def prefix(value, axis, join, neutral):
    place = lax.axis_index(axis)
    gathered = jax.tree.map(
        lambda a, kind: lax.all_gather(a.astype(kind), axis), value, (jnp.bfloat16, jnp.bfloat16)
    )
    state = jax.tree.map(lambda a, e: jnp.zeros_like(a) + jnp.asarray(e, a.dtype), value, neutral)

    def one(hop, state):
        return join(
            state,
            jax.tree.map(
                lambda a, own: lax.dynamic_index_in_dim(a, hop, 0, False).astype(own.dtype),
                gathered,
                value,
            ),
        )

    return lax.fori_loop(0, place, one, state)


def prefix_2(value, axis, join, neutral):
    count = lax.axis_size(axis)
    place = lax.axis_index(axis)
    ahead = count - 1 - place
    gathered = jax.tree.map(
        lambda a, kind: lax.all_gather(a.astype(kind), axis),
        value,
        jax.tree.map(lambda a: jnp.bfloat16 if a.dtype == jnp.float32 else a.dtype, value),
    )
    state = jax.tree.map(lambda a, e: jnp.zeros_like(a) + jnp.asarray(e, a.dtype), value, neutral)

    def one(hop, state):
        source = count - 1 - hop
        return join(
            state,
            jax.tree.map(
                lambda a, own: lax.dynamic_index_in_dim(a, source, 0, False).astype(own.dtype),
                gathered,
                value,
            ),
        )

    return lax.fori_loop(0, ahead, one, state)


def rms_norm(values, gain):
    scaling = lax.rsqrt(jnp.mean(values * values, axis=-1, keepdims=True) + eps_norm)
    return values * scaling * gain


def matmul_high(left_op, right_op):
    return jnp.dot(left_op, right_op, precision=highest, preferred_element_type=jnp.float32)


def matmul_low(left_op, right_op):
    return jnp.dot(left_op, right_op, preferred_element_type=jnp.float32)


def matmul_tn(left_op, right_op):
    return lax.dot_general(
        left_op, right_op, (((0,), (0,)), ((), ())), preferred_element_type=jnp.float32
    )


def matmul_nt(left_op, right_op):
    return lax.dot_general(
        left_op, right_op, (((1,), (1,)), ((), ())), preferred_element_type=jnp.float32
    )


def rotate(values, positions):
    half_dim = values.shape[-1] // 2
    frequency = rope_base ** (-(jnp.arange(half_dim).astype(jnp.float32) * 2.0 / values.shape[-1]))
    angles = positions.astype(jnp.float32)[:, None] * frequency[None, :]
    cosine = jnp.cos(angles)[:, None, :]
    sine_part = jnp.sin(angles)[:, None, :]
    front_half = values[..., :half_dim]
    back_half = values[..., half_dim:]
    return jnp.concatenate(
        [front_half * cosine - back_half * sine_part, back_half * cosine + front_half * sine_part],
        axis=-1,
    )


def conv_silu(conv_input, edge_rows, edge_seg, segment, weight, offsets):
    tap_count = weight.shape[0]
    row_total = conv_input.shape[0]
    padded = jnp.concatenate([edge_rows, conv_input], axis=0)
    seg_pad = jnp.concatenate([edge_seg, segment], axis=0)
    summed = jnp.zeros_like(conv_input) + offsets[None, :]
    for tap_index in range(tap_count):
        shifted = padded[tap_index : tap_index + row_total]
        same_doc = (seg_pad[tap_index : tap_index + row_total] == segment)[:, None]
        summed = summed + jnp.where(same_doc, shifted * weight[tap_index][None, :], 0.0)
    return jax.nn.silu(summed)


def decay_sums(step_size, a_neg):
    return jnp.cumsum(step_size * a_neg[None, :], axis=0)


def intra_block(x_heads, bmat, cmat, step_size, cumulative, segment):
    ordering = jnp.arange(x_heads.shape[0])
    same_doc = (segment[:, None] == segment[None, :]) & (ordering[:, None] >= ordering[None, :])
    products = matmul_high(cmat, bmat.T)
    gaps = jnp.where(
        same_doc[:, :, None], cumulative[:, None, :] - cumulative[None, :, :], far_negative
    )
    weights = jnp.exp(gaps) * products[:, :, None] * step_size[None, :, :]
    return jnp.einsum("tsh,shp->thp", weights, x_heads, precision=highest)


def read_state(cmat, cumulative, segment, seg_prev, state_in):
    is_live = (segment == seg_prev)[:, None, None]
    carried = jnp.einsum("tn,hpn->thp", cmat, state_in, precision=highest)
    return jnp.where(is_live, carried * jnp.exp(cumulative)[:, :, None], 0.0)


def block_state(x_heads, bmat, step_size, cumulative, segment, seg_prev):
    kept_rows = (segment == segment[-1])[:, None]
    weights = jnp.where(kept_rows, jnp.exp(cumulative[-1][None, :] - cumulative) * step_size, 0.0)
    own_state = jnp.einsum("th,thp,tn->hpn", weights, x_heads, bmat, precision=highest)
    decays = jnp.where(segment[-1] == seg_prev, jnp.exp(cumulative[-1]), 0.0)
    return (own_state, decays)


def chain_step(earlier, later):
    return (earlier[0] * later[0], later[0][:, None, None] * earlier[1] + later[1])


def keep_same(current):
    return current


def add_trees(first_tree, second_tree):
    if first_tree is None:
        return second_tree
    return jax.tree.map(jnp.add, first_tree, second_tree)


def on_device(
    inputs,
    cotangent,
    doc_starts,
    norm_one,
    mixer_in,
    conv_weight,
    conv_bias,
    dt_bias,
    a_log,
    d_skip,
    ssm_gain,
    mixer_out,
    attn_in,
    attn_out,
    norm_two,
    ffn_in,
    ffn_out,
):
    head_count = lax.axis_size("head")
    blk_count = lax.axis_size("blk")
    blk_index = lax.axis_index("blk")
    head_index = lax.axis_index("head")
    tok_rows = inputs.shape[1]
    edge_total = head_count * tok_rows
    tokens_all = edge_total * blk_count
    longest = min(MAXLEN, tokens_all // 2)
    reach_blocks = (longest + edge_total - 2) // edge_total
    heads_dev = MHEADS // head_count
    x_cols = heads_dev * MHDIM
    conv_cols = x_cols + 2 * STATE
    query_dev = QHEADS // head_count
    query_cols = query_dev * HDIM
    group_size = QHEADS // KVHEADS
    kv_pick = np.array([slot * query_dev // group_size for slot in range(head_count)])
    scaling = HDIM ** (-0.5)
    lag_rows = CONVK - 1
    token_pos = (blk_index * head_count + head_index) * tok_rows + jnp.arange(
        tok_rows, dtype=jnp.int32
    )
    block_pos = blk_index * edge_total + jnp.arange(edge_total, dtype=jnp.int32)
    edge_pos = blk_index * edge_total - lag_rows + jnp.arange(lag_rows, dtype=jnp.int32)
    block_first = blk_index * edge_total
    chain_start = (
        jnp.ones((heads_dev,), jnp.float32),
        jnp.zeros((heads_dev, MHDIM, STATE), jnp.float32),
    )

    def spread_rows(matrix):
        return jnp.broadcast_to(matrix[:, None, :], (tok_rows, head_count, matrix.shape[1]))

    def split_cols(matrix):
        return matrix.reshape(tok_rows, head_count, matrix.shape[1] // head_count)

    def prepare(proj_m, proj_a):
        gate_z = proj_m[:, :DI]
        conv_x = proj_m[:, DI : 2 * DI].reshape(tok_rows, head_count, x_cols)
        conv_bc = jnp.broadcast_to(
            proj_m[:, 2 * DI : 2 * DI + 2 * STATE][:, None, :], (tok_rows, head_count, 2 * STATE)
        )
        conv_in = jnp.concatenate([conv_x, conv_bc], axis=2)
        dt_raw = proj_m[:, 2 * DI + 2 * STATE :].reshape(tok_rows, head_count, heads_dev)
        queries = rotate(proj_a[:, : QHEADS * HDIM].reshape(tok_rows, QHEADS, HDIM), token_pos)
        key_part = rotate(
            proj_a[:, QHEADS * HDIM : (QHEADS + KVHEADS) * HDIM].reshape(tok_rows, KVHEADS, HDIM),
            token_pos,
        )
        value_part = proj_a[:, (QHEADS + KVHEADS) * HDIM :].reshape(tok_rows, KVHEADS, HDIM)
        key_value = jnp.concatenate([key_part, value_part], axis=2)[:, kv_pick, :]
        qkv = jnp.concatenate(
            [queries.reshape(tok_rows, head_count, query_cols), key_value], axis=2
        )
        return (gate_z, conv_in, qkv, dt_raw)

    def gate_norm(mixed, gate_z, gain):
        return rms_norm(mixed * jax.nn.silu(gate_z), gain)

    def swiglu(gate_up):
        return jax.nn.silu(gate_up[:, :FF]) * gate_up[:, FF:]

    def micro_step(values_in, cot_in, starts, weights):
        gain_one, w_mix_in, w_mix_out, w_attn_in, w_attn_out, gain_two, w_ffn_in, w_ffn_out = (
            weights
        )
        resid = values_in.astype(jnp.float32)

        def seg_of(positions):
            return jnp.sum((starts[None, :] <= positions[:, None]).astype(jnp.int32), axis=1)

        segment = seg_of(block_pos)
        edge_seg = jnp.where(edge_pos >= 0, seg_of(edge_pos), -1)
        seg_prev = edge_seg[-1]
        first_norm, norm_pull = jax.vjp(rms_norm, resid, gain_one.astype(jnp.float32))
        normed_low = first_norm.astype(jnp.bfloat16)
        proj_m = matmul_low(normed_low, w_mix_in)
        proj_a = matmul_low(normed_low, w_attn_in)
        (gate_z, conv_in, qkv, dt_raw), prep_pull = jax.vjp(prepare, proj_m, proj_a)
        sent = (
            lax.all_to_all(
                conv_in.astype(jnp.bfloat16).reshape(1, tok_rows, head_count, conv_cols),
                "head",
                split_axis=2,
                concat_axis=0,
                tiled=True,
            ),
            lax.all_to_all(
                qkv.astype(jnp.bfloat16).reshape(1, tok_rows, head_count, query_cols + 2 * HDIM),
                "head",
                split_axis=2,
                concat_axis=0,
                tiled=True,
            ),
            lax.all_to_all(
                dt_raw.astype(jnp.bfloat16).reshape(1, tok_rows, head_count, heads_dev),
                "head",
                split_axis=2,
                concat_axis=0,
                tiled=True,
            ),
        )
        conv_heads = sent[0].reshape(edge_total, conv_cols)
        qkv_heads = sent[1].reshape(edge_total, query_cols + 2 * HDIM)
        dt_heads = sent[2].reshape(edge_total, heads_dev).astype(jnp.float32)
        query_heads = qkv_heads[:, :query_cols]
        kv_heads = qkv_heads[:, query_cols:]
        edge_in = shifted_2(conv_heads[edge_total - lag_rows :], "blk", 1)

        def conv_part(conv_input, edge_rows, weight_all, offset_all):
            weight = jnp.concatenate(
                [
                    lax.dynamic_slice_in_dim(weight_all, head_index * x_cols, x_cols, 1),
                    weight_all[:, DI:],
                ],
                axis=1,
            )
            offsets = jnp.concatenate(
                [
                    lax.dynamic_slice_in_dim(offset_all, head_index * x_cols, x_cols, 0),
                    offset_all[DI:],
                ],
                axis=0,
            )
            return conv_silu(conv_input, edge_rows, edge_seg, segment, weight, offsets)

        convolved, conv_pull = jax.vjp(
            conv_part,
            conv_heads.astype(jnp.float32),
            edge_in.astype(jnp.float32),
            conv_weight,
            conv_bias,
        )

        def ssm_inputs(conv_out, dt_in, bias_all, alog_all):
            x_heads = conv_out[:, :x_cols].reshape(edge_total, heads_dev, MHDIM)
            bmat = conv_out[:, x_cols : x_cols + STATE]
            cmat = conv_out[:, x_cols + STATE :]
            step_size = jax.nn.softplus(
                dt_in
                + lax.dynamic_slice_in_dim(bias_all, head_index * heads_dev, heads_dev)[None, :]
            )
            a_neg = -jnp.exp(lax.dynamic_slice_in_dim(alog_all, head_index * heads_dev, heads_dev))
            return (x_heads, bmat, cmat, step_size, decay_sums(step_size, a_neg))

        def mamba_out(conv_out, dt_in, bias_all, alog_all, skip_all, state_in):
            x_heads, bmat, cmat, step_size, cumulative = ssm_inputs(
                conv_out, dt_in, bias_all, alog_all
            )
            skip_gain = lax.dynamic_slice_in_dim(skip_all, head_index * heads_dev, heads_dev)
            result = (
                intra_block(x_heads, bmat, cmat, step_size, cumulative, segment)
                + read_state(cmat, cumulative, segment, seg_prev, state_in)
                + skip_gain[None, :, None] * x_heads
            )
            return result.reshape(edge_total, x_cols)

        def mamba_state(conv_out, dt_in, bias_all, alog_all):
            x_heads, bmat, cmat, step_size, cumulative = ssm_inputs(
                conv_out, dt_in, bias_all, alog_all
            )
            return block_state(x_heads, bmat, step_size, cumulative, segment, seg_prev)

        (own_state, decays), state_pull = jax.vjp(mamba_state, convolved, dt_heads, dt_bias, a_log)
        state_in = prefix((decays, own_state), "blk", chain_step, chain_start)[1]
        mamba_y, out_pull = jax.vjp(
            mamba_out, convolved, dt_heads, dt_bias, a_log, d_skip, state_in
        )
        query_three = query_heads.reshape(edge_total, query_dev, HDIM)

        def attend_block(running, key_value, first_row):
            key_pos = first_row + jnp.arange(edge_total, dtype=jnp.int32)
            key_seg = seg_of(key_pos)

            def attend_compute(current):
                run_max, run_sum, accum = current
                key_rows = key_value[:, :HDIM]
                value_rows = key_value[:, HDIM:]
                allowed = (segment[:, None] == key_seg[None, :]) & (
                    block_pos[:, None] >= key_pos[None, :]
                )
                scores = (
                    jnp.einsum(
                        "qhd,kd->hqk", query_three, key_rows, preferred_element_type=jnp.float32
                    )
                    * scaling
                )
                scores = jnp.where(allowed[None], scores, far_negative)
                new_max = jnp.maximum(run_max, jnp.max(scores, axis=2))
                weights = jnp.where(allowed[None], jnp.exp(scores - new_max[:, :, None]), 0.0)
                rescale = jnp.exp(run_max - new_max)
                new_sum = run_sum * rescale + jnp.sum(weights, axis=2)
                update = jnp.einsum(
                    "hqk,kd->hqd",
                    weights.astype(jnp.bfloat16),
                    value_rows,
                    preferred_element_type=jnp.float32,
                )
                return (new_max, new_sum, accum * rescale[:, :, None] + update)

            empty = (first_row < 0) | (key_seg[-1] < segment[0])
            return lax.cond(empty, keep_same, attend_compute, running)

        attn_start = (
            jnp.full((query_dev, edge_total), far_negative, jnp.float32),
            jnp.zeros((query_dev, edge_total), jnp.float32),
            jnp.zeros((query_dev, edge_total, HDIM), jnp.float32),
        )
        local_attn = attend_block(attn_start, kv_heads, block_first)

        def earlier_step(carry, step_index):
            moving, running = carry
            moving = shifted_2(moving, "blk", 1)
            return (
                (
                    moving,
                    attend_block(running, moving, block_first - (step_index + 1) * edge_total),
                ),
                moving,
            )

        step_list = jnp.arange(reach_blocks, dtype=jnp.int32)
        attn_carry, kept_kv = lax.scan(earlier_step, (kv_heads, local_attn), step_list)
        run_max, run_sum, accum = attn_carry[1]
        attn_heads = accum / run_sum[:, :, None]
        log_total = run_max + jnp.log(run_sum)
        attn_rows = jnp.transpose(attn_heads, (1, 0, 2)).reshape(edge_total, query_cols)
        back = (
            lax.all_to_all(
                mamba_y.astype(jnp.bfloat16).reshape(head_count, tok_rows, 1, x_cols),
                "head",
                split_axis=0,
                concat_axis=2,
                tiled=True,
            ),
            lax.all_to_all(
                attn_rows.astype(jnp.bfloat16).reshape(head_count, tok_rows, 1, query_cols),
                "head",
                split_axis=0,
                concat_axis=2,
                tiled=True,
            ),
        )
        mixed_low = back[0].reshape(tok_rows, DI)
        attn_low = back[1].reshape(tok_rows, QHEADS * HDIM)
        gated, gate_pull = jax.vjp(gate_norm, mixed_low.astype(jnp.float32), gate_z, ssm_gain)
        gated_low = gated.astype(jnp.bfloat16)
        hidden = resid + matmul_low(gated_low, w_mix_out) + matmul_low(attn_low, w_attn_out)
        second_norm, norm_two_pull = jax.vjp(rms_norm, hidden, gain_two.astype(jnp.float32))
        second_low = second_norm.astype(jnp.bfloat16)
        gate_up = matmul_low(second_low, w_ffn_in)
        activated, swiglu_pull = jax.vjp(swiglu, gate_up)
        activated_low = activated.astype(jnp.bfloat16)
        result = hidden + matmul_low(activated_low, w_ffn_out)
        grad_act = matmul_nt(cot_in, w_ffn_out)
        grad_gate_up = swiglu_pull(grad_act)[0].astype(jnp.bfloat16)
        grad_second = matmul_nt(grad_gate_up, w_ffn_in)
        grad_hid_part, grad_gain_two = norm_two_pull(grad_second)
        grad_hidden = cot_in.astype(jnp.float32) + grad_hid_part
        hidden_low = grad_hidden.astype(jnp.bfloat16)
        grad_gated = matmul_nt(hidden_low, w_mix_out)
        grad_attn_tok = matmul_nt(hidden_low, w_attn_out)
        grad_mixed, grad_gate_z, grad_ssm_gain = gate_pull(grad_gated)
        returned = (
            lax.all_to_all(
                grad_mixed.astype(jnp.bfloat16).reshape(1, tok_rows, head_count, x_cols),
                "head",
                split_axis=2,
                concat_axis=0,
                tiled=True,
            ),
            lax.all_to_all(
                grad_attn_tok.astype(jnp.bfloat16).reshape(1, tok_rows, head_count, query_cols),
                "head",
                split_axis=2,
                concat_axis=0,
                tiled=True,
            ),
        )
        grad_y = returned[0].reshape(edge_total, x_cols).astype(jnp.float32)
        grad_attn_rows = returned[1].reshape(edge_total, query_cols)
        grad_three = grad_attn_rows.reshape(edge_total, query_dev, HDIM)
        correction = jnp.einsum("qhd,hqd->hq", grad_three.astype(jnp.float32), attn_heads)

        def query_grad_block(running, key_value, first_row):
            key_pos = first_row + jnp.arange(edge_total, dtype=jnp.int32)
            key_seg = seg_of(key_pos)

            def query_compute(current):
                key_rows = key_value[:, :HDIM]
                value_rows = key_value[:, HDIM:]
                allowed = (segment[:, None] == key_seg[None, :]) & (
                    block_pos[:, None] >= key_pos[None, :]
                )
                scores = (
                    jnp.einsum(
                        "qhd,kd->hqk", query_three, key_rows, preferred_element_type=jnp.float32
                    )
                    * scaling
                )
                probs = jnp.where(allowed[None], jnp.exp(scores - log_total[:, :, None]), 0.0)
                grad_probs = jnp.einsum(
                    "qhd,kd->hqk", grad_three, value_rows, preferred_element_type=jnp.float32
                )
                grad_scores = (probs * (grad_probs - correction[:, :, None])).astype(jnp.bfloat16)
                return (
                    current
                    + jnp.einsum(
                        "hqk,kd->qhd", grad_scores, key_rows, preferred_element_type=jnp.float32
                    )
                    * scaling
                )

            empty = (first_row < 0) | (key_seg[-1] < segment[0])
            return lax.cond(empty, keep_same, query_compute, running)

        local_query = query_grad_block(
            jnp.zeros((edge_total, query_dev, HDIM), jnp.float32), kv_heads, block_first
        )

        def earlier_back_step(running, pair):
            step_index, moving = pair
            return (
                query_grad_block(running, moving, block_first - (step_index + 1) * edge_total),
                None,
            )

        grad_query = lax.scan(earlier_back_step, local_query, (step_list, kept_kv))[0]
        key_local = kv_heads[:, :HDIM]
        value_local = kv_heads[:, HDIM:]

        def key_grad_block(running, parts, first_row):
            query_rows, grad_rows, lse_rows, corr_rows = parts
            query_pos = first_row + jnp.arange(edge_total, dtype=jnp.int32)
            query_seg = seg_of(query_pos)

            def key_compute(current):
                allowed = (query_seg[:, None] == segment[None, :]) & (
                    query_pos[:, None] >= block_pos[None, :]
                )
                query_part = query_rows.reshape(edge_total, query_dev, HDIM)
                grad_part = grad_rows.reshape(edge_total, query_dev, HDIM)
                scores = (
                    jnp.einsum(
                        "qhd,kd->hqk", query_part, key_local, preferred_element_type=jnp.float32
                    )
                    * scaling
                )
                probs = jnp.where(
                    allowed[None], jnp.exp(scores - jnp.transpose(lse_rows)[:, :, None]), 0.0
                )
                grad_value = jnp.einsum(
                    "hqk,qhd->kd",
                    probs.astype(jnp.bfloat16),
                    grad_part,
                    preferred_element_type=jnp.float32,
                )
                grad_probs = jnp.einsum(
                    "qhd,kd->hqk", grad_part, value_local, preferred_element_type=jnp.float32
                )
                grad_scores = (probs * (grad_probs - jnp.transpose(corr_rows)[:, :, None])).astype(
                    jnp.bfloat16
                )
                grad_key = (
                    jnp.einsum(
                        "hqk,qhd->kd", grad_scores, query_part, preferred_element_type=jnp.float32
                    )
                    * scaling
                )
                return current + jnp.concatenate([grad_key, grad_value], axis=1)

            empty = (first_row >= tokens_all) | (query_seg[0] > segment[-1])
            return lax.cond(empty, keep_same, key_compute, running)

        query_parts = (
            query_heads,
            grad_attn_rows,
            jnp.transpose(log_total),
            jnp.transpose(correction),
        )
        local_kv = key_grad_block(
            jnp.zeros((edge_total, 2 * HDIM), jnp.float32), query_parts, block_first
        )

        def later_step(step_index, carry):
            moving, running = carry
            moving = (
                shifted_2(moving[0], "blk", -1),
                shifted_2(moving[1], "blk", -1),
                shifted_2(moving[2].astype(jnp.bfloat16), "blk", -1).astype(jnp.float32),
                shifted_2(moving[3].astype(jnp.bfloat16), "blk", -1).astype(jnp.float32),
            )
            return (
                moving,
                key_grad_block(running, moving, block_first + (step_index + 1) * edge_total),
            )

        grad_kv = lax.fori_loop(0, reach_blocks, later_step, (query_parts, local_kv))[1]
        grad_conv_a, grad_dt_a, grad_bias_a, grad_alog_a, grad_skip, grad_state = out_pull(grad_y)
        adjoint = prefix_2((decays, grad_state), "blk", chain_step, chain_start)[1]
        grad_decay = jnp.sum(adjoint * state_in, axis=(1, 2))
        grad_conv_b, grad_dt_b, grad_bias_b, grad_alog_b = state_pull((adjoint, grad_decay))
        grad_conv_in, grad_edge, grad_conv_w, grad_conv_bias = conv_pull(grad_conv_a + grad_conv_b)
        from_next = shifted_2(grad_edge, "blk", -1)
        grad_conv_in = grad_conv_in.at[edge_total - lag_rows :].add(from_next)
        grad_dt = (grad_dt_a + grad_dt_b).astype(jnp.bfloat16)
        grad_qkv = jnp.concatenate(
            [grad_query.reshape(edge_total, query_cols), grad_kv], axis=1
        ).astype(jnp.bfloat16)
        home = (
            lax.all_to_all(
                grad_conv_in.astype(jnp.bfloat16).reshape(head_count, tok_rows, 1, conv_cols),
                "head",
                split_axis=0,
                concat_axis=2,
                tiled=True,
            ),
            lax.all_to_all(
                grad_qkv.reshape(head_count, tok_rows, 1, query_cols + 2 * HDIM),
                "head",
                split_axis=0,
                concat_axis=2,
                tiled=True,
            ),
            lax.all_to_all(
                grad_dt.reshape(head_count, tok_rows, 1, heads_dev),
                "head",
                split_axis=0,
                concat_axis=2,
                tiled=True,
            ),
        )
        grad_proj_m, grad_proj_a = prep_pull(
            (
                grad_gate_z,
                home[0].reshape(tok_rows, head_count, conv_cols).astype(jnp.float32),
                home[1].reshape(tok_rows, head_count, query_cols + 2 * HDIM).astype(jnp.float32),
                home[2].reshape(tok_rows, head_count, heads_dev).astype(jnp.float32),
            )
        )
        proj_m_low = grad_proj_m.astype(jnp.bfloat16)
        proj_a_low = grad_proj_a.astype(jnp.bfloat16)
        grad_normed = matmul_nt(proj_m_low, w_mix_in) + matmul_nt(proj_a_low, w_attn_in)
        grad_resid_part, grad_gain_one = norm_pull(grad_normed)
        grad_input = grad_hidden + grad_resid_part
        operands = (
            lax.all_to_all(
                spread_rows(activated_low), "head", split_axis=1, concat_axis=0, tiled=True
            ),
            lax.all_to_all(
                spread_rows(second_low), "head", split_axis=1, concat_axis=0, tiled=True
            ),
            lax.all_to_all(spread_rows(gated_low), "head", split_axis=1, concat_axis=0, tiled=True),
            lax.all_to_all(spread_rows(attn_low), "head", split_axis=1, concat_axis=0, tiled=True),
            lax.all_to_all(
                spread_rows(normed_low), "head", split_axis=1, concat_axis=0, tiled=True
            ),
            lax.all_to_all(split_cols(cot_in), "head", split_axis=1, concat_axis=0, tiled=True),
            lax.all_to_all(
                split_cols(grad_gate_up), "head", split_axis=1, concat_axis=0, tiled=True
            ),
            lax.all_to_all(split_cols(hidden_low), "head", split_axis=1, concat_axis=0, tiled=True),
            lax.all_to_all(split_cols(proj_m_low), "head", split_axis=1, concat_axis=0, tiled=True),
            lax.all_to_all(split_cols(proj_a_low), "head", split_axis=1, concat_axis=0, tiled=True),
        )
        flat = [member.reshape(edge_total, member.shape[2]) for member in operands]
        grad_ffn_out = matmul_tn(flat[0], flat[5])
        grad_ffn_in = matmul_tn(flat[1], flat[6])
        grad_mix_out = matmul_tn(flat[2], flat[7])
        grad_attn_out = matmul_tn(flat[3], flat[7])
        grad_mix_in = matmul_tn(flat[4], flat[8])
        grad_attn_in = matmul_tn(flat[4], flat[9])
        big_grads = (
            grad_ffn_out,
            grad_ffn_in,
            grad_mix_out,
            grad_attn_out,
            grad_mix_in,
            grad_attn_in,
        )
        small_grads = (
            grad_conv_w,
            grad_conv_bias,
            grad_bias_a + grad_bias_b,
            grad_alog_a + grad_alog_b,
            grad_skip,
            grad_ssm_gain,
            grad_gain_one,
            grad_gain_two,
        )
        return (result, grad_input, big_grads, small_grads)

    results = []
    input_grads = []
    totals = None
    weights = (
        lax.all_gather(norm_one, ("blk", "head"), axis=0, tiled=True),
        lax.all_gather(mixer_in, ("blk", "head"), axis=0, tiled=True),
        lax.all_gather(mixer_out, ("blk", "head"), axis=1, tiled=True),
        lax.all_gather(attn_in, ("blk", "head"), axis=0, tiled=True),
        lax.all_gather(attn_out, ("blk", "head"), axis=1, tiled=True),
        lax.all_gather(norm_two, ("blk", "head"), axis=0, tiled=True),
        lax.all_gather(ffn_in, ("blk", "head"), axis=0, tiled=True),
        lax.all_gather(ffn_out, ("blk", "head"), axis=1, tiled=True),
    )
    for micro_index in range(MB):
        result, grad_input, big_grads, small_grads = micro_step(
            inputs[micro_index], cotangent[micro_index], doc_starts[micro_index], weights
        )
        results.append(result)
        input_grads.append(grad_input)
        totals = add_trees(totals, (big_grads, small_grads))
    big_grads = totals[0]
    reduced = (
        lax.psum_scatter(big_grads[0], "blk", scatter_dimension=0, tiled=True),
        lax.psum_scatter(big_grads[1], "blk", scatter_dimension=0, tiled=True),
        lax.psum_scatter(big_grads[2], "blk", scatter_dimension=0, tiled=True),
        lax.psum_scatter(big_grads[3], "blk", scatter_dimension=0, tiled=True),
        lax.psum_scatter(big_grads[4], "blk", scatter_dimension=0, tiled=True),
        lax.psum_scatter(big_grads[5], "blk", scatter_dimension=0, tiled=True),
    )
    summed = lax.psum(totals[1], ("blk", "head"))
    totals = (reduced, summed)
    reduced = totals[0]
    summed = totals[1]
    return (
        jnp.stack(results),
        jnp.stack(input_grads),
        summed[6],
        reduced[4],
        summed[0],
        summed[1],
        summed[2],
        summed[3],
        summed[4],
        summed[5],
        reduced[2],
        reduced[5],
        reduced[3],
        summed[7],
        reduced[1],
        reduced[0],
    )


def solution(mesh):
    placed = (
        P(None, ("blk", "head"), None),
        P(None, ("blk", "head"), None),
        P(),
        P(("blk", "head")),
        P(("blk", "head"), None),
        P(),
        P(),
        P(),
        P(),
        P(),
        P(),
        P(None, ("blk", "head")),
        P(("blk", "head"), None),
        P(None, ("blk", "head")),
        P(("blk", "head")),
        P(("blk", "head"), None),
        P(None, ("blk", "head")),
    )
    return jax.shard_map(
        on_device,
        mesh=mesh,
        in_specs=placed,
        out_specs=(
            P(None, ("blk", "head"), None),
            P(None, ("blk", "head"), None),
            P(),
            P("blk", "head"),
            P(),
            P(),
            P(),
            P(),
            P(),
            P(),
            P("blk", "head"),
            P("blk", "head"),
            P("blk", "head"),
            P(),
            P("blk", "head"),
            P("blk", "head"),
        ),
        check_vma=False,
    )
```

profile of v0, /device:TPU:0, one launch (start us, length us, event | category | flops | bytes accessed | tf_op | source)
XLA Modules:
  0.0 1196.2 jit_solution(13349936568036444359)
XLA Ops:
  23.9 42.1 %all-reduce.63 = (bf16[1024]{0:T(1024)(128)(2,1)S(1)}, bf16[1024]{0:T(1024)(128)(2,1)S(1)}) all-reduce(bf16[1024]{0:T(1024)(128)(2,1)S(1)} %dynamic-update-slice.15, bf16[1024]{0:T(1024)(128)(2,1)S(1)} %dynamic-update-slice.16), channel_id=1, replica_groups=mesh['blk'=8,'head'=4] {'blk','head'}, use_global_device_ids=true, to_apply=%add.60 | all-reduce | flops 2048 | bytes 8192
  90.6 4.0 all-to-all-done.3
  98.1 4.4 all-to-all-done.8
  106.2 31.6 %while.181 = (s32[]{:T(128)}, bf16[256,128]{0,1:T(8,128)(2,1)S(1)}, f32[2,256]{1,0:T(2,128)S(1)}, f32[2,256]{1,0:T(2,128)S(1)}, f32[2,256,64]{1,2,0:T(8,128)S(1)...) while((s32[]{:T(128)}, bf16[256,128]{0,1:T(8,128)(2,1)S(1)}, ...), condition=%wide.region_38.40_spmd.clone.clone, body=%wide.region_32.39_spmd.clone.clone.sunk | while | flops 34999304 | bytes 2798007 | solution.py:412
  106.2 3.9 collective-permute-start.1
  114.0 4.3 collective-permute-start.1
  129.5 4.4 collective-permute-start.1
  143.3 32.2 %while.180 = (s32[]{:T(128)}, bf16[256,128]{0,1:T(8,128)(2,1)S(1)}, f32[2,256]{1,0:T(2,128)S(1)}, f32[2,256]{1,0:T(2,128)S(1)}, f32[2,256,64]{1,2,0:T(8,128)S(1)...) while((s32[]{:T(128)}, bf16[256,128]{0,1:T(8,128)(2,1)S(1)}, ...), condition=%wide.region_18.20_spmd.clone.clone, body=%wide.region_12.19_spmd.clone.clone.sunk | while | flops 34999304 | bytes 2798007 | solution.py:412
  150.5 4.2 collective-permute-start
  158.6 4.1 collective-permute-start
  166.6 5.1 collective-permute-start
  190.2 10.9 all-gather.13.cloned.1.call-done
  201.2 4.5 fusion.530
  238.2 19.0 %all-gather.4 = bf16[8,1,6]{2,1,0:T(2,128)(2,1)S(1)} all-gather(bf16[1,1,6]{2,1,0:T(2,128)(2,1)S(1)} %bitcast.1487), channel_id=1, replica_groups=mesh['blk'=8,'head'=4] {'blk'}, dimensions={0}, use_global_device_ids=true | all-gather | bytes 108 | tf_op jit(solution)/shard_map/all_gather | solution.py:35
  257.2 16.1 %all-gather.5 = bf16[8,1,6]{2,1,0:T(2,128)(2,1)S(1)} all-gather(bf16[1,1,6]{2,1,0:T(2,128)(2,1)S(1)} %bitcast.1486), channel_id=1, replica_groups=mesh['blk'=8,'head'=4] {'blk'}, dimensions={0}, use_global_device_ids=true | all-gather | bytes 108 | tf_op jit(solution)/shard_map/all_gather | solution.py:35
  274.1 3.9 collective-permute-start.10
  284.8 35.3 %all-gather = bf16[48,64,128]{2,1,0:T(8,128)(2,1)} all-gather(bf16[6,64,128]{2,1,0:T(8,128)(2,1)S(1)} %convolution_convert_fusion.3), channel_id=2, replica_groups=mesh['blk'=8,'head'=4] {'blk'}, dimensions={0}, use_global_device_ids=true | all-gather | bytes 884736 | tf_op jit(solution)/shard_map/all_gather | solution.py:35
  325.4 4.0 all-to-all-start.2
  333.4 38.6 %all-gather.1 = bf16[48,64,128]{2,1,0:T(8,128)(2,1)} all-gather(bf16[6,64,128]{2,1,0:T(8,128)(2,1)S(1)} %convolution_convert_fusion.2), channel_id=3, replica_groups=mesh['blk'=8,'head'=4] {'blk'}, dimensions={0}, use_global_device_ids=true | all-gather | bytes 884736 | tf_op jit(solution)/shard_map/all_gather | solution.py:35
  381.1 5.9 all-to-all-done.7
  398.3 6.6 fusion.533
  404.9 13.3 %all-gather.23.cloned.1.call-done = bf16[2048,1024]{0,1:T(8,128)(2,1)} async-done(((bf16[2048,32]{0,1:T(8,128)(2,1)}), bf16[2048,1024]{0,1:T(8,128)(2,1)}) %all-gather.23.cloned.1.call-update) | async-done | bytes 4194320 | tf_op jit(solution)/shard_map/all_gather | solution.py:693
  418.2 4.3 fusion.420
  423.6 6.8 multiply_reduce_fusion.19
  467.0 15.2 %while.182 = (s32[]{:T(128)}, f32[256,2,64]{0,2,1:T(8,128)S(1)}, s32[4]{0:T(128)S(1)}, s32[]{:T(128)}, s32[1,2]{1,0:T(1,128)S(1)}, /*index=5*/s32[256]{0:T(256)S...) while((s32[]{:T(128)}, f32[256,2,64]{0,2,1:T(8,128)S(1)}, ...), condition=%wide.region_62.64_spmd.clone.clone, body=%wide.region_58.63_spmd.clone.clone.sunk | while | flops 51382280 | bytes 1818999 | solution.py:517
  485.0 15.2 %while.184 = (s32[]{:T(128)}, f32[256,2,64]{0,2,1:T(8,128)S(1)}, s32[4]{0:T(128)S(1)}, s32[]{:T(128)}, s32[1,2]{1,0:T(1,128)S(1)}, /*index=5*/s32[256]{0:T(256)S...) while((s32[]{:T(128)}, f32[256,2,64]{0,2,1:T(8,128)S(1)}, ...), condition=%wide.region_94.96_spmd.clone.clone, body=%wide.region_90.95_spmd.clone.clone.sunk | while | flops 51382280 | bytes 1818999 | solution.py:517
  502.4 57.3 %while.183 = (s32[]{:T(128)}, bf16[256,128]{0,1:T(8,128)(2,1)S(1)}, bf16[256,128]{0,1:T(8,128)(2,1)S(1)}, f32[256,2]{0,1:T(2,128)S(1)}, f32[256,2]{0,1:T(2,128)S...) while((s32[]{:T(128)}, bf16[256,128]{0,1:T(8,128)(2,1)S(1)}, ...), condition=%wide.region_69.71_spmd.clone.clone, body=%wide.region_65.70_spmd.clone.clone.sunk | while | flops 68309000 | bytes 3379691 | solution.py:587
  510.2 4.3 collective-permute-done.4
  525.4 4.7 collective-permute-done.4
  540.9 4.3 collective-permute-done.4
  565.7 53.4 %while.185 = (s32[]{:T(128)}, bf16[256,128]{0,1:T(8,128)(2,1)S(1)}, bf16[256,128]{0,1:T(8,128)(2,1)S(1)}, f32[256,2]{0,1:T(2,128)S(1)}, f32[256,2]{0,1:T(2,128)S...) while((s32[]{:T(128)}, bf16[256,128]{0,1:T(8,128)(2,1)S(1)}, ...), condition=%wide.region_101.103_spmd.clone.clone, body=%wide.region_97.102_spmd.clone.clone.sunk | while | flops 68309000 | bytes 3379691 | solution.py:587
  624.1 3.9 all-to-all-done.27
  631.7 4.3 all-to-all-done.25
  647.3 4.5 all-to-all-done.19
  658.8 6.3 all-to-all-done.20
  671.8 6.6 all-to-all-done.22
  695.9 4.5 all-to-all-start.26
  707.9 4.2 all-to-all-done.26
  725.1 4.0 all-to-all-done.24
  746.5 39.2 %all-gather.3 = bf16[48,64,128]{2,1,0:T(8,128)(2,1)S(1)} all-gather(bf16[6,64,128]{2,1,0:T(8,128)(2,1)S(1)} %convolution_convert_fusion), channel_id=5, replica_groups=mesh['blk'=8,'head'=4] {'blk'}, dimensions={0}, use_global_device_ids=true | all-gather | bytes 884736 | tf_op jit(solution)/shard_map/all_gather | solution.py:57
  785.7 5.6 while.179
  796.1 3.9 all-to-all-start.39
  801.1 33.2 %all-gather.2 = bf16[48,64,128]{2,1,0:T(8,128)(2,1)S(1)} all-gather(bf16[6,64,128]{2,1,0:T(8,128)(2,1)S(1)} %convolution_convert_fusion.1), channel_id=4, replica_groups=mesh['blk'=8,'head'=4] {'blk'}, dimensions={0}, use_global_device_ids=true | all-gather | bytes 884736 | tf_op jit(solution)/shard_map/all_gather | solution.py:57
  834.3 5.9 while.178
  885.0 4.5 all-to-all-start.38
  889.5 7.6 reduce-window.56
  897.3 7.6 reduce-window.54
  905.1 7.6 reduce-window.46
  912.9 7.6 reduce-window.50
  922.2 4.3 all-to-all-start.36
  930.8 10.2 all-to-all-done.36
  965.5 5.1 all-to-all-done.17
  974.2 6.6 all-to-all-done.12
  987.0 6.7 all-to-all-done.21
  993.8 4.1 all-to-all-start.23
  999.9 6.3 all-to-all-done.23
  1016.0 8.0 all-to-all-done.32
  1027.7 8.8 all-to-all-done.33
  1036.4 11.2 all_to_all.542
  1055.0 5.8 all-to-all-done.34
  1060.8 4.9 bitcast_add_fusion
  1077.2 5.8 fusion.538
  1087.3 45.3 %all-reduce.62 = (f32[1024]{0:T(1024)}, f32[4,1792]{1,0:T(4,128)}, f32[1792]{0:T(1024)}, f32[24]{0:T(128)}, f32[24]{0:T(128)}, /*index=5*/f32[24]{0:T(128)}, f32[1536]{0:T(1024)}, f32[1024]{0:T(1024)}) all-reduce(f32[1024]{0:T(1024)S(1)} %add.887, f32[4,1792]{1,0:T(4,128)S(1)} %add.889, ...), channel_id=1, replica_groups=mesh['blk'=8,'head'=4] {'blk','head'}, use_global_device_ids=true, to_apply=%region_106.108 | all-reduce | flops 12616 | bytes 100928 | tf_op jit(solution)/shard_map/psum | solution.py:711
  1134.9 54.0 %reduce-scatter.15.cloned.1.call-done = f32[128,1024]{1,0:T(8,128)} async-done(((f32[1024,1024]{1,0:T(8,128)}), f32[128,1024]{1,0:T(8,128)}) %reduce-scatter.15.cloned.1.call-update) | async-done | bytes 524304 | tf_op jit(solution)/shard_map/reduce_scatter | solution.py:705
  (1576 shorter events, 543.8 us)
Async XLA Ops:
  7.2 73.0 %all-gather.17.cloned.1.call-start = ((), (), s32[]{:S(2)}) async-start(), calls=%async_computation.48 | async-start | bytes 1622016 | tf_op jit(solution)/shard_map/all_gather | solution.py:689
  8.0 178.7 %all-gather.19.cloned.1.call-start = ((), (), s32[]{:S(2)}) async-start(), calls=%async_computation.49 | async-start | bytes 1081344 | tf_op jit(solution)/shard_map/all_gather | solution.py:690
  8.7 192.5 %all-gather.13.cloned.1.call-start = ((), (), s32[]{:S(2)}) async-start(), calls=%async_computation.46 | async-start | bytes 7299072 | tf_op jit(solution)/shard_map/all_gather | solution.py:687
  9.4 381.3 %all-gather.15.cloned.1.call-start = ((), (), s32[]{:S(2)}) async-start(), calls=%async_computation.47 | async-start | bytes 3244032 | tf_op jit(solution)/shard_map/all_gather | solution.py:688
  10.0 388.3 %all-gather.21.cloned.1.call-start = ((), (), s32[]{:S(2)}) async-start(), calls=%async_computation.50 | async-start | bytes 8650752 | tf_op jit(solution)/shard_map/all_gather | solution.py:692
  10.6 407.6 %all-gather.23.cloned.1.call-start = ((), (), s32[]{:S(2)}) async-start(), calls=%async_computation.51 | async-start | bytes 4325376 | tf_op jit(solution)/shard_map/all_gather | solution.py:693
  138.8 38.3 %all-to-all-start.9 = ((bf16[4,64,1,128]{3,1,2,0:T(8,128)(2,1)}), bf16[4,64,1,128]{3,1,2,0:T(8,128)(2,1)S(1)}, u32[]{:S(2)}, u32[]{:S(2)}) async-start(bf16[4,64,1,128]{3,1,2,0:T(8,128)(2,1)} %copy.782), calls=%async_computation.9 | async-start | bytes 131072 | tf_op jit(solution)/shard_map/all_to_all | solution.py:425
  166.6 8.8 collective-permute-start
  222.5 12.0 %all-to-all-start = ((bf16[1,64,4,640]{3,1,0,2:T(8,128)(2,1)}), bf16[1,64,4,640]{3,1,0,2:T(8,128)(2,1)S(1)}, u32[]{:S(2)}, u32[]{:S(2)}) async-start(bf16[1,64,4,640]{3,1,0,2:T(8,128)(2,1)} %pad_maximum_fusion.6), calls=%async_computation | async-start | bytes 655360 | tf_op jit(solution)/shard_map/all_to_all | solution.py:270
  234.5 43.5 %all-to-all-start.5 = ((bf16[1,64,4,640]{3,1,0,2:T(8,128)(2,1)}), bf16[1,64,4,640]{3,1,0,2:T(8,128)(2,1)S(1)}, u32[]{:S(2)}, u32[]{:S(2)}) async-start(bf16[1,64,4,640]{3,1,0,2:T(8,128)(2,1)} %pad_maximum_fusion.7), calls=%async_computation.5 | async-start | bytes 655360 | tf_op jit(solution)/shard_map/all_to_all | solution.py:270
  278.1 51.4 %collective-permute-start.11 = (bf16[3,640]{1,0:T(4,128)(2,1)S(1)}, bf16[3,640]{1,0:T(4,128)(2,1)}, u32[]{:S(2)}, u32[]{:S(2)}) collective-permute-start(bf16[3,640]{1,0:T(4,128)(2,1)S(1)} %slice.603), channel_id=1, source_target_pairs={{0,4},{4,8},{8,12},{12,16},{16,20},{20,24},{24,28},{1,5},{5,9},{9,... | collective-permute-start | bytes 11528 | tf_op jit(solution)/shard_map/ppermute | solution.py:29
  325.4 50.9 %all-to-all-start.2 = ((bf16[4,64,1,384]{3,1,2,0:T(8,128)(2,1)}), bf16[4,64,1,384]{3,1,2,0:T(8,128)(2,1)}, u32[]{:S(2)}, u32[]{:S(2)}) async-start(bf16[4,64,1,384]{3,1,2,0:T(8,128)(2,1)} %copy.751), calls=%async_computation.2 | async-start | bytes 393216 | tf_op jit(solution)/shard_map/all_to_all | solution.py:418
  376.3 10.7 all-to-all-start.7
  460.3 101.2 %all-to-all-start.31 = ((bf16[64,4,512]{2,0,1:T(8,128)(2,1)}), bf16[64,4,512]{2,0,1:T(8,128)(2,1)S(1)}, u32[]{:S(2)}, u32[]{:S(2)}) async-start(bf16[64,4,512]{2,0,1:T(8,128)(2,1)} %broadcast_in_dim.606), calls=%async_computation.34 | async-start | bytes 524288 | tf_op jit(solution)/shard_map/all_to_all | solution.py:643
  502.4 14.1 %collective-permute-start.2 = (bf16[256,128]{0,1:T(8,128)(2,1)S(1)}, bf16[256,128]{0,1:T(8,128)(2,1)S(1)}, u32[]{:S(2)}, u32[]{:S(2)}) collective-permute-start(bf16[256,128]{0,1:T(8,128)(2,1)S(1)} %get-tuple-element.3551), channel_id=1, source_target_pairs={{4,0},{8,4},{12,8},{16,12},{20,16},{24,20},{28,24},{5,1},{9,5},{13... | collective-permute-start | bytes 196616 | tf_op jit(solution)/shard_map/while/body/eval_jaxpr/ppermute | solution.py:29
  503.8 12.7 %collective-permute-start.3 = (bf16[256,128]{0,1:T(8,128)(2,1)S(1)}, bf16[256,128]{0,1:T(8,128)(2,1)S(1)}, u32[]{:S(2)}, u32[]{:S(2)}) collective-permute-start(bf16[256,128]{0,1:T(8,128)(2,1)S(1)} %get-tuple-element.3552), channel_id=1, source_target_pairs={{4,0},{8,4},{12,8},{16,12},{20,16},{24,20},{28,24},{5,1},{9,5},{13... | collective-permute-start | bytes 196616 | tf_op jit(solution)/shard_map/while/body/eval_jaxpr/ppermute | solution.py:29
  505.1 9.4 collective-permute-start.4
  506.4 10.0 collective-permute-start.5
  517.6 14.4 %collective-permute-start.2 = (bf16[256,128]{0,1:T(8,128)(2,1)S(1)}, bf16[256,128]{0,1:T(8,128)(2,1)S(1)}, u32[]{:S(2)}, u32[]{:S(2)}) collective-permute-start(bf16[256,128]{0,1:T(8,128)(2,1)S(1)} %get-tuple-element.3551), channel_id=1, source_target_pairs={{4,0},{8,4},{12,8},{16,12},{20,16},{24,20},{28,24},{5,1},{9,5},{13... | collective-permute-start | bytes 196616 | tf_op jit(solution)/shard_map/while/body/eval_jaxpr/ppermute | solution.py:29
  518.9 13.1 %collective-permute-start.3 = (bf16[256,128]{0,1:T(8,128)(2,1)S(1)}, bf16[256,128]{0,1:T(8,128)(2,1)S(1)}, u32[]{:S(2)}, u32[]{:S(2)}) collective-permute-start(bf16[256,128]{0,1:T(8,128)(2,1)S(1)} %get-tuple-element.3552), channel_id=1, source_target_pairs={{4,0},{8,4},{12,8},{16,12},{20,16},{24,20},{28,24},{5,1},{9,5},{13... | collective-permute-start | bytes 196616 | tf_op jit(solution)/shard_map/while/body/eval_jaxpr/ppermute | solution.py:29
  520.2 9.8 collective-permute-start.4
  521.6 10.4 collective-permute-start.5
  533.1 14.0 %collective-permute-start.2 = (bf16[256,128]{0,1:T(8,128)(2,1)S(1)}, bf16[256,128]{0,1:T(8,128)(2,1)S(1)}, u32[]{:S(2)}, u32[]{:S(2)}) collective-permute-start(bf16[256,128]{0,1:T(8,128)(2,1)S(1)} %get-tuple-element.3551), channel_id=1, source_target_pairs={{4,0},{8,4},{12,8},{16,12},{20,16},{24,20},{28,24},{5,1},{9,5},{13... | collective-permute-start | bytes 196616 | tf_op jit(solution)/shard_map/while/body/eval_jaxpr/ppermute | solution.py:29
  534.4 12.7 %collective-permute-start.3 = (bf16[256,128]{0,1:T(8,128)(2,1)S(1)}, bf16[256,128]{0,1:T(8,128)(2,1)S(1)}, u32[]{:S(2)}, u32[]{:S(2)}) collective-permute-start(bf16[256,128]{0,1:T(8,128)(2,1)S(1)} %get-tuple-element.3552), channel_id=1, source_target_pairs={{4,0},{8,4},{12,8},{16,12},{20,16},{24,20},{28,24},{5,1},{9,5},{13... | collective-permute-start | bytes 196616 | tf_op jit(solution)/shard_map/while/body/eval_jaxpr/ppermute | solution.py:29
  535.8 9.4 collective-permute-start.4
  537.1 10.1 collective-permute-start.5
  548.3 11.3 collective-permute-start.2
  549.6 10.0 collective-permute-start.3
  562.3 57.9 %all-to-all-start.30 = ((bf16[64,4,512]{2,0,1:T(8,128)(2,1)}), bf16[64,4,512]{2,0,1:T(8,128)(2,1)S(1)}, u32[]{:S(2)}, u32[]{:S(2)}) async-start(bf16[64,4,512]{2,0,1:T(8,128)(2,1)} %broadcast_in_dim.605), calls=%async_computation.33 | async-start | bytes 524288 | tf_op jit(solution)/shard_map/all_to_all | solution.py:643
  565.7 12.2 %collective-permute-start.6 = (bf16[256,128]{0,1:T(8,128)(2,1)S(1)}, bf16[256,128]{0,1:T(8,128)(2,1)S(1)}, u32[]{:S(2)}, u32[]{:S(2)}) collective-permute-start(bf16[256,128]{0,1:T(8,128)(2,1)S(1)} %get-tuple-element.3638), channel_id=1, source_target_pairs={{4,0},{8,4},{12,8},{16,12},{20,16},{24,20},{28,24},{5,1},{9,5},{13... | collective-permute-start | bytes 196616 | tf_op jit(solution)/shard_map/while/body/eval_jaxpr/ppermute | solution.py:29
  567.0 10.9 collective-permute-start.7
  579.1 13.1 %collective-permute-start.6 = (bf16[256,128]{0,1:T(8,128)(2,1)S(1)}, bf16[256,128]{0,1:T(8,128)(2,1)S(1)}, u32[]{:S(2)}, u32[]{:S(2)}) collective-permute-start(bf16[256,128]{0,1:T(8,128)(2,1)S(1)} %get-tuple-element.3638), channel_id=1, source_target_pairs={{4,0},{8,4},{12,8},{16,12},{20,16},{24,20},{28,24},{5,1},{9,5},{13... | collective-permute-start | bytes 196616 | tf_op jit(solution)/shard_map/while/body/eval_jaxpr/ppermute | solution.py:29
  580.4 11.8 collective-permute-start.7
  583.0 9.1 collective-permute-start.9
  593.3 13.3 %collective-permute-start.6 = (bf16[256,128]{0,1:T(8,128)(2,1)S(1)}, bf16[256,128]{0,1:T(8,128)(2,1)S(1)}, u32[]{:S(2)}, u32[]{:S(2)}) collective-permute-start(bf16[256,128]{0,1:T(8,128)(2,1)S(1)} %get-tuple-element.3638), channel_id=1, source_target_pairs={{4,0},{8,4},{12,8},{16,12},{20,16},{24,20},{28,24},{5,1},{9,5},{13... | collective-permute-start | bytes 196616 | tf_op jit(solution)/shard_map/while/body/eval_jaxpr/ppermute | solution.py:29
  594.6 12.0 %collective-permute-start.7 = (bf16[256,128]{0,1:T(8,128)(2,1)S(1)}, bf16[256,128]{0,1:T(8,128)(2,1)S(1)}, u32[]{:S(2)}, u32[]{:S(2)}) collective-permute-start(bf16[256,128]{0,1:T(8,128)(2,1)S(1)} %get-tuple-element.3639), channel_id=1, source_target_pairs={{4,0},{8,4},{12,8},{16,12},{20,16},{24,20},{28,24},{5,1},{9,5},{13... | collective-permute-start | bytes 196616 | tf_op jit(solution)/shard_map/while/body/eval_jaxpr/ppermute | solution.py:29
  595.9 8.7 collective-permute-start.8
  597.2 9.3 collective-permute-start.9
  607.7 11.3 collective-permute-start.6
  609.0 10.0 collective-permute-start.7
  639.3 495.5 %reduce-scatter.13.cloned.1.call-start = ((), (), s32[]{:S(2)}) async-start(), calls=%async_computation.55 | async-start | bytes 589824 | tf_op jit(solution)/shard_map/reduce_scatter | solution.py:707
  652.7 12.4 %all-to-all-start.20 = ((bf16[64,4,1024]{2,0,1:T(8,128)(2,1)}), bf16[64,4,1024]{2,0,1:T(8,128)(2,1)S(1)}, u32[]{:S(2)}, u32[]{:S(2)}) async-start(bf16[64,4,1024]{2,0,1:T(8,128)(2,1)} %broadcast_in_dim.601), calls=%async_computation.20 | async-start | bytes 1048576 | tf_op jit(solution)/shard_map/all_to_all | solution.py:644
  666.1 12.3 %all-to-all-start.22 = ((bf16[64,4,1024]{2,0,1:T(8,128)(2,1)}), bf16[64,4,1024]{2,0,1:T(8,128)(2,1)S(1)}, u32[]{:S(2)}, u32[]{:S(2)}) async-start(bf16[64,4,1024]{2,0,1:T(8,128)(2,1)} %broadcast_in_dim.602), calls=%async_computation.22 | async-start | bytes 1048576 | tf_op jit(solution)/shard_map/all_to_all | solution.py:644
  695.9 16.2 %all-to-all-start.26 = ((bf16[64,4,1536]{2,0,1:T(8,128)(2,1)}), bf16[64,4,1536]{2,0,1:T(8,128)(2,1)}, u32[]{:S(2)}, u32[]{:S(2)}) async-start(bf16[64,4,1536]{2,0,1:T(8,128)(2,1)} %broadcast_in_dim.604), calls=%async_computation.27 | async-start | bytes 1572864 | tf_op jit(solution)/shard_map/all_to_all | solution.py:642
  700.4 434.5 %reduce-scatter.11.cloned.1.call-start = ((), (), s32[]{:S(2)}) async-start(), calls=%async_computation.54 | async-start | bytes 884736 | tf_op jit(solution)/shard_map/reduce_scatter | solution.py:709
  714.0 15.1 %all-to-all-start.24 = ((bf16[64,4,1536]{2,0,1:T(8,128)(2,1)}), bf16[64,4,1536]{2,0,1:T(8,128)(2,1)S(1)}, u32[]{:S(2)}, u32[]{:S(2)}) async-start(bf16[64,4,1536]{2,0,1:T(8,128)(2,1)} %broadcast_in_dim.603), calls=%async_computation.25 | async-start | bytes 1572864 | tf_op jit(solution)/shard_map/all_to_all | solution.py:642
  732.4 402.4 %reduce-scatter.9.cloned.1.call-start = ((), (), s32[]{:S(2)}) async-start(), calls=%async_computation.53 | async-start | bytes 1769472 | tf_op jit(solution)/shard_map/reduce_scatter | solution.py:706
  737.8 58.3 %all-to-all-start.10 = ((bf16[1,64,4,384]{3,1,0,2:T(8,128)(2,1)}), bf16[1,64,4,384]{3,1,0,2:T(8,128)(2,1)S(1)}, u32[]{:S(2)}, u32[]{:S(2)}) async-start(bf16[1,64,4,384]{3,1,0,2:T(8,128)(2,1)} %copy.784), calls=%async_computation.10 | async-start | bytes 393216 | tf_op jit(solution)/shard_map/all_to_all | solution.py:454
  796.1 79.6 %all-to-all-start.39 = ((bf16[64,4,256]{2,0,1:T(8,128)(2,1)}), bf16[64,4,256]{2,0,1:T(8,128)(2,1)}, u32[]{:S(2)}, u32[]{:S(2)}) async-start(bf16[64,4,256]{2,0,1:T(8,128)(2,1)} %copy.855), calls=%async_computation.44 | async-start | bytes 262144 | tf_op jit(solution)/shard_map/all_to_all | solution.py:647
  869.5 88.8 %collective-permute-start.13 = (f32[3,640]{1,0:T(4,128)}, f32[3,640]{1,0:T(4,128)S(1)}, u32[]{:S(2)}, u32[]{:S(2)}) collective-permute-start(f32[3,640]{1,0:T(4,128)} %pad_add_fusion.6), channel_id=1, source_target_pairs={{4,0},{8,4},{12,8},{16,12},{20,16},{24,20},{28,24},{5,1},{9,5},{13... | collective-permute-start | bytes 23048 | tf_op jit(solution)/shard_map/ppermute | solution.py:29
  885.0 36.0 %all-to-all-start.38 = ((bf16[64,4,2048]{2,0,1:T(8,128)(2,1)}), bf16[64,4,2048]{2,0,1:T(8,128)(2,1)}, u32[]{:S(2)}, u32[]{:S(2)}) async-start(bf16[64,4,2048]{2,0,1:T(8,128)(2,1)} %broadcast_in_dim.610), calls=%async_computation.43 | async-start | bytes 2097152 | tf_op jit(solution)/shard_map/all_to_all | solution.py:636
  922.2 18.8 %all-to-all-start.36 = ((bf16[64,4,2048]{2,0,1:T(8,128)(2,1)}), bf16[64,4,2048]{2,0,1:T(8,128)(2,1)}, u32[]{:S(2)}, u32[]{:S(2)}) async-start(bf16[64,4,2048]{2,0,1:T(8,128)(2,1)} %broadcast_in_dim.609), calls=%async_computation.41 | async-start | bytes 2097152 | tf_op jit(solution)/shard_map/all_to_all | solution.py:636
  941.0 10.2 all-to-all-start.16
  944.2 190.7 %reduce-scatter.17.cloned.1.call-start = ((), (), s32[]{:S(2)}) async-start(), calls=%async_computation.57 | async-start | bytes 2359296 | tf_op jit(solution)/shard_map/reduce_scatter | solution.py:704
  949.1 15.0 %collective-permute-start.12 = (f32[3,640]{1,0:T(4,128)S(1)}, f32[3,640]{1,0:T(4,128)S(1)}, u32[]{:S(2)}, u32[]{:S(2)}) collective-permute-start(f32[3,640]{1,0:T(4,128)S(1)} %pad_add_fusion.7), channel_id=1, source_target_pairs={{4,0},{8,4},{12,8},{16,12},{20,16},{24,20},{28,24},{5,1},{9,5},{13... | collective-permute-start | bytes 23048 | tf_op jit(solution)/shard_map/ppermute | solution.py:29
  960.4 10.2 all-to-all-start.17
  970.6 10.2 all-to-all-start.12
  982.2 11.6 all-to-all-start.21
  993.8 12.3 %all-to-all-start.23 = ((bf16[64,4,838]{2,0,1:T(8,128)(2,1)}), bf16[64,4,838]{2,0,1:T(8,128)(2,1)}, u32[]{:S(2)}, u32[]{:S(2)}) async-start(bf16[64,4,838]{2,0,1:T(8,128)(2,1)} %copy.847), calls=%async_computation.23 | async-start | bytes 917504 | tf_op jit(solution)/shard_map/all_to_all | solution.py:652
  998.0 137.0 %reduce-scatter.7.cloned.1.call-start = ((), (), s32[]{:S(2)}) async-start(), calls=%async_computation.52 | async-start | bytes 3870720 | tf_op jit(solution)/shard_map/reduce_scatter | solution.py:708
  1011.6 12.4 %all-to-all-start.32 = ((bf16[64,4,1024]{2,0,1:T(8,128)(2,1)}), bf16[64,4,1024]{2,0,1:T(8,128)(2,1)S(1)}, u32[]{:S(2)}, u32[]{:S(2)}) async-start(bf16[64,4,1024]{2,0,1:T(8,128)(2,1)} %broadcast_in_dim.607), calls=%async_computation.36 | async-start | bytes 1048576 | tf_op jit(solution)/shard_map/all_to_all | solution.py:639
  1024.0 12.4 %all-to-all-start.33 = ((bf16[64,4,1024]{2,0,1:T(8,128)(2,1)}), bf16[64,4,1024]{2,0,1:T(8,128)(2,1)S(1)}, u32[]{:S(2)}, u32[]{:S(2)}) async-start(bf16[64,4,1024]{2,0,1:T(8,128)(2,1)} %bitcast.1295), calls=%async_computation.37 | async-start | bytes 1048576 | tf_op jit(solution)/shard_map/all_to_all | solution.py:648
  1048.5 12.3 %all-to-all-start.34 = ((bf16[64,4,1024]{2,0,1:T(8,128)(2,1)}), bf16[64,4,1024]{2,0,1:T(8,128)(2,1)S(1)}, u32[]{:S(2)}, u32[]{:S(2)}) async-start(bf16[64,4,1024]{2,0,1:T(8,128)(2,1)} %broadcast_in_dim.608), calls=%async_computation.38 | async-start | bytes 1048576 | tf_op jit(solution)/shard_map/all_to_all | solution.py:639
  1052.0 137.0 %reduce-scatter.15.cloned.1.call-start = ((), (), s32[]{:S(2)}) async-start(), calls=%async_computation.56 | async-start | bytes 4718592 | tf_op jit(solution)/shard_map/reduce_scatter | solution.py:705
  (321 other events, 6176.6 us)
Sparse Core Ops, SparseCore 0:
  10.9 57.7 all-gather.16
  71.6 52.6 all-gather.18
  127.3 73.8 all-gather.12
  203.9 58.1 all-gather.14
  264.8 87.9 all-gather.20
  355.5 62.6 all-gather.22
  644.1 69.7 reduce-scatter.12
  718.2 62.3 reduce-scatter.10
  784.6 66.3 reduce-scatter.8
  949.3 67.5 reduce-scatter.16
  1021.5 75.5 reduce-scatter.6
  1101.1 87.7 reduce-scatter.14
where the time goes:
time: 1210 us; the launch traced here: 1200 us
  blocking collectives  280 us (23%)
  waiting for transfers between devices  262 us (22%)
  starting transfers between devices  223 us (18%)
  matrix products  132 us (11%)
  local copies, waits for them, and re-layouts  123 us (10%)
  other arithmetic  103 us (9%)
  loops' own time  45.3 us (4%)
  between operations  27.7 us (2%)
    all_gather x4, blocking collectives, prefix(): lax.all_gather(a.astype(kind), axis)  109 us
    ppermute x44, starting transfers between devices, shifted_2(): lax.ppermute(value, axis, [(source, source + steps) for source in range(f...  83.2 us
    all_gather x2, blocking collectives, prefix_2(): lax.all_gather(a.astype(kind), axis)  72.3 us
    reduce_scatter x1, waiting for transfers between devices, on_device(): lax.psum_scatter(big_grads[1], 'blk', scatter_dimension=0, tiled=True)  54 us
    psum x1, blocking collectives, on_device(): summed = lax.psum(totals[1], ('blk', 'head'))  45.3 us
    unnamed x1, blocking collectives  42.1 us
    ppermute x44, waiting for transfers between devices, shifted_2(): lax.ppermute(value, axis, [(source, source + steps) for source in range(f...  41.5 us
    another operation x17, other arithmetic  35.2 us
  transfers between devices with their start and end apart: 95, of which 48 were waited for; matrix products, arithmetic and copies ran while one was open for 27% of the time, Pallas kernels for 0%

commit v1 on v0

v1 whole, which is shorter than its diff:
```python
import functools

import jax
import jax.numpy as jnp
import numpy as np
from jax import lax
from jax.experimental import pallas as pl
from jax.experimental.pallas import tpu as pltpu
from jax.sharding import PartitionSpec as P

MHEADS = 24
MHDIM = 64
STATE = 128
QHEADS = 8
HDIM = 64
FF = 2048
DI = 1536
D = 1024
MAXLEN = 4096
NH = 4
HG = MHEADS // NH
XC = HG * MHDIM
FG = FF // NH
W1C = 2 * XC + 3 * 128
WRC = 2 * FG + XC + 128 + FG
LAG = 16
EPS = 1e-5
FAR = -1e30
SCALE = HDIM**-0.5
MESH = pl.DeviceIdType.MESH
BF = jnp.bfloat16
F32 = jnp.float32
VMEM_LIMIT = 60 * 2**20
high = lax.Precision.HIGHEST


def nn(a, b):
    return lax.dot_general(a, b, (((1,), (0,)), ((), ())), preferred_element_type=F32)


def nt(a, b):
    return lax.dot_general(a, b, (((1,), (1,)), ((), ())), preferred_element_type=F32)


def tn(a, b):
    return lax.dot_general(a, b, (((0,), (0,)), ((), ())), preferred_element_type=F32)


def other(index, step):
    return index + step - 2 * step * lax.rem(index // step, 2)


def copy_to(src, dst, send, recv, where):
    return pltpu.make_async_remote_copy(
        src_ref=src, dst_ref=dst, send_sem=send, recv_sem=recv, device_id=where, device_id_type=MESH
    )


def barrier(edges):
    sem = pltpu.get_barrier_semaphore()
    for there, where in edges:
        if there is True:
            pl.semaphore_signal(sem, inc=1, device_id=where, device_id_type=MESH)
        else:

            @pl.when(there)
            def _():
                pl.semaphore_signal(sem, inc=1, device_id=where, device_id_type=MESH)

    total = 0
    for there, _ in edges:
        total = total + (1 if there is True else there.astype(jnp.int32))
    pl.semaphore_wait(sem, total)


def lanes(shape):
    return lax.broadcasted_iota(jnp.int32, shape, len(shape) - 1)


def rows_of(shape):
    return lax.broadcasted_iota(jnp.int32, shape, len(shape) - 2)


def sigmoid(v):
    return 1.0 / (1.0 + jnp.exp(-v))


def widen(cols, first, count=HG, width=MHDIM):
    return jnp.concatenate(
        [
            jnp.broadcast_to(cols[:, first + i : first + i + 1], (cols.shape[0], width))
            for i in range(count)
        ],
        axis=1,
    )


class LineGather:
    def __init__(self, piece, b, h, nb, sems):
        self.piece, self.h, self.nz = piece, h, nb // 2
        self.z, self.x = b // 2, lax.rem(b, 2)
        self.line_recv, self.send_r, self.send_l, self.x_send, self.x_recv = sems

    @staticmethod
    def scratch(nb):
        return [pltpu.SemaphoreType.DMA((nb // 2,))] * 5

    def at(self, z, x=None):
        return self.piece(2 * z + (self.x if x is None else x))

    def to_x(self, z):
        return copy_to(
            self.at(z), self.at(z), self.x_send.at[z], self.x_recv.at[z], (2 * self.z + 1 - self.x, self.h)
        )

    def to_z(self, z, way):
        send = self.send_r if way > 0 else self.send_l
        return copy_to(
            self.at(z), self.at(z), send.at[z], self.line_recv.at[z], (2 * (self.z + way) + self.x, self.h)
        )

    def begin(self):
        self.to_x(self.z).start()
        self.hop(0)

    def hop(self, s):
        @pl.when((self.z - s >= 0) & (self.z + 1 < self.nz))
        def _():
            self.to_z(self.z - s, 1).start()

        @pl.when((self.z + s < self.nz) & (self.z >= 1))
        def _():
            self.to_z(self.z + s, -1).start()

    def advance(self, s):
        left, right = self.z - 1 - s, self.z + 1 + s

        @pl.when(left >= 0)
        def _():
            self.to_z(left, 1).wait_recv()
            self.to_x(left).start()

        @pl.when(right < self.nz)
        def _():
            self.to_z(right, -1).wait_recv()
            self.to_x(right).start()

        if s + 1 < self.nz - 1:
            self.hop(s + 1)

    def finish(self):
        for z in range(self.nz):
            copy_to(
                self.at(z, 1 - self.x),
                self.at(z, 1 - self.x),
                self.x_send.at[z],
                self.x_recv.at[z],
                (2 * self.z + 1 - self.x, self.h),
            ).wait_recv()
        for z in range(self.nz):
            self.to_x(z).wait_send()

            @pl.when((z <= self.z) & (self.z + 1 < self.nz))
            def _():
                self.to_z(z, 1).wait_send()

            @pl.when((z >= self.z) & (self.z >= 1))
            def _():
                self.to_z(z, -1).wait_send()

    def edges(self):
        return line_edges(2 * self.z + self.x, self.h, 2 * self.nz)


def line_edges(b, h, nb):
    return [
        (True, (other(b, 1), h)),
        (b >= 2, (b - 2, h)),
        (b + 2 < nb, (b + 2, h)),
    ]


def head_edges(b, h):
    return [(True, (b, other(h, 1))), (True, (b, other(h, 2))), (True, (b, NH - 1 - h))]


class HeadGather:
    def __init__(self, rows, b, h, sems):
        self.rows, self.b, self.h = rows, b, h
        self.send, self.recv = sems

    @staticmethod
    def scratch():
        return [pltpu.SemaphoreType.DMA((3,))] * 2

    def copy(self, i):
        pair, across = other(self.h, 1), other(self.h, 2)
        rows = self.rows(self.h if i < 2 else across)
        return copy_to(rows, rows, self.send.at[i], self.recv.at[i], (self.b, across if i == 1 else pair))

    def begin(self):
        self.copy(1).start()
        self.copy(0).start()

    def forward(self):
        self.copy(1).wait_recv()
        self.copy(2).start()

    def finish(self):
        self.copy(0).wait_recv()
        self.copy(2).wait_recv()
        for i in range(3):
            self.copy(i).wait_send()


class HeadScatter:
    def __init__(self, full, b, h, bufs, sems):
        self.full, self.b, self.h = full, b, h
        self.send_c, self.recv_c, self.send_y, self.recv_y = bufs
        self.send, self.recv = sems

    @staticmethod
    def scratch(rows, width=D):
        return [
            pltpu.VMEM((2, 2, rows, width), BF),
            pltpu.VMEM((2, 2, rows, width), BF),
            pltpu.VMEM((2, rows, width), BF),
            pltpu.VMEM((2, rows, width), BF),
            pltpu.SemaphoreType.DMA((2,)),
            pltpu.SemaphoreType.DMA((2,)),
        ]

    def copy(self, i):
        src, dst = ((self.send_c, self.recv_c), (self.send_y, self.recv_y))[i]
        return copy_to(src, dst, self.send.at[i], self.recv.at[i], (self.b, other(self.h, i + 1)))

    def begin(self):
        core = lax.rem(self.h, 2)
        for y in range(2):
            for m in range(2):
                self.send_c[y, m] = self.full(m, 2 * y + 1 - core).astype(BF)
        self.copy(0).start()

    def middle(self):
        core, y = lax.rem(self.h, 2), self.h // 2
        self.copy(0).wait_recv()
        for m in range(2):
            self.send_y[m] = (
                self.full(m, 2 * (1 - y) + core) + self.recv_c[1 - y, m].astype(F32)
            ).astype(BF)
        self.copy(1).start()

    def finish(self):
        self.copy(1).wait_recv()
        self.copy(0).wait_send()
        self.copy(1).wait_send()

    def result(self, m):
        y = self.h // 2
        return self.full(m, self.h) + self.recv_c[y, m].astype(F32) + self.recv_y[m].astype(F32)


def place():
    return lax.axis_index("blk"), lax.axis_index("head")


def rotate_pair(v, cosine, sine):
    lane = lax.rem(lanes(v.shape), HDIM)
    front = lane < HDIM // 2
    partner = jnp.where(front, pltpu.roll(v, 128 - HDIM // 2, 1), pltpu.roll(v, HDIM // 2, 1))
    return v * cosine + jnp.where(front, -partner, partner) * sine


def rope_tables(freq_ref, b, rows, ref_cos, ref_sin):
    pos = (b * rows + rows_of((rows, 128))).astype(F32)
    angle = pos * freq_ref[...]
    ref_cos[...] = jnp.cos(angle)
    ref_sin[...] = jnp.sin(angle)


def front_kernel(
    nb, T, local_pieces,
    x_ref, cot_ref, w1p_ref, wrp_ref, freq_ref,
    normed_ref, gate_ref, xin_ref, bc_ref, q_ref, kv_ref, dt_ref, cotg_ref, w1_ref, wr_ref, gains_ref,
    cos_ref, sin_ref,
    xg, sx0, sx1, sc0, sc1, sp, rp, l0, l1, l2, l3, l4, k0, k1, k2, k3, k4, halo_s, halo_r, own_s, pair_s, pair_r,
):
    b, h = place()
    tok = T // NH
    rpb = D // nb
    piece = rpb // NH
    barrier(
        head_edges(b, h)
        + line_edges(b, h, nb)
        + [((h == NH - 1) & (b + 1 < nb), (b + 1, jnp.int32(i))) for i in range(NH)]
        + [(b >= 1, (b - 1, jnp.int32(NH - 1)))]
    )
    gather_x = HeadGather(lambda i: xg.at[:, pl.ds(LAG + i * tok, tok)], b, h, (sx0, sx1))
    gather_c = HeadGather(lambda i: cotg_ref.at[:, pl.ds(i * tok, tok)], b, h, (sc0, sc1))
    line1 = LineGather(lambda i: w1_ref.at[pl.ds(i * rpb, rpb)], b, h, nb, (l0, l1, l2, l3, l4))
    line2 = LineGather(lambda i: wr_ref.at[pl.ds(i * rpb, rpb)], b, h, nb, (k0, k1, k2, k3, k4))

    sent = []
    if local_pieces:
        for n, (src, dst) in enumerate(((w1p_ref, w1_ref), (wrp_ref, wr_ref))):
            for i, to in enumerate((other(h, 1), other(h, 2), NH - 1 - h)):
                mine = dst.at[pl.ds(b * rpb + h * piece, piece)]
                sent.append(copy_to(src.at[to], mine, sp.at[3 * n + i], rp.at[3 * n + i], (b, to)))
            if n == 0:
                for c in sent:
                    c.start()
                w1_ref[pl.ds(b * rpb + h * piece, piece), :] = w1p_ref[h]
    else:
        w1_ref[pl.ds(b * rpb, rpb), :] = w1p_ref[...]
    for m in range(2):
        xg[m, pl.ds(LAG + h * tok, tok), :] = x_ref[m]
        cotg_ref[m, pl.ds(h * tok, tok), :] = cot_ref[m]
    gather_x.begin()

    def halo(i):
        return copy_to(
            x_ref.at[:, pl.ds(tok - LAG, LAG)], xg.at[:, pl.ds(0, LAG)], halo_s.at[i], halo_r.at[0], (b + 1, jnp.int32(i))
        )

    @pl.when((h == NH - 1) & (b + 1 < nb))
    def _():
        for i in range(NH):
            halo(i).start()

    @pl.when(b == 0)
    def _():
        xg[:, 0:LAG, :] = jnp.zeros((2, LAG, D), BF)

    if local_pieces:
        for i in range(3):
            sent[i].wait_recv()
    line1.begin()
    gather_c.begin()
    if local_pieces:
        for i in range(3):
            sent[3 + i].start()
        own = pltpu.make_async_copy(wrp_ref.at[h], wr_ref.at[pl.ds(b * rpb + h * piece, piece)], own_s.at[0])
    else:
        own = pltpu.make_async_copy(wrp_ref, wr_ref.at[pl.ds(b * rpb, rpb)], own_s.at[0])
    own.start()
    rope_tables(freq_ref, b, T, cos_ref, sin_ref)
    gather_x.forward()
    gather_c.forward()
    gather_x.finish()

    @pl.when(b >= 1)
    def _():
        halo(0).wait_recv()

    @pl.when((h == NH - 1) & (b + 1 < nb))
    def _():
        for i in range(NH):
            halo(i).wait_send()

    own.wait()
    if local_pieces:
        for i in range(3):
            sent[3 + i].wait_recv()
    for s in range(nb // 2 - 1):
        line1.advance(s)
    line1.finish()
    line2.begin()

    last = w1_ref[:, W1C - 128 :].astype(F32).T
    gains_ref[...] = last[HDIM + HG + 2 - 8 : HDIM + HG + 2]
    n1 = gains_ref[6:7, :]
    for m in range(2):
        v = xg[m].astype(F32)
        scale = lax.rsqrt(jnp.mean(v * v, axis=1, keepdims=True) + EPS)
        normed_ref[m] = (v * scale * n1).astype(BF)
    core = lax.rem(h, 2)
    small = 2 * XC
    lane = lanes((T, 128))
    kv, dt = [], []
    for m in range(2):
        bc = nn(normed_ref[m], w1_ref[:, small : small + 128])
        bc_ref[m, :, pl.ds(pl.multiple_of(core * 128, 128), 128)] = bc.astype(BF)
        kv.append(nn(normed_ref[m, LAG:], w1_ref[:, small + 256 : small + 384]))
    packed = jnp.where(lane < HDIM, kv[0], pltpu.roll(kv[1], HDIM, 1))
    turned = rotate_pair(packed, cos_ref[...], sin_ref[...])
    kv_ref[core] = jnp.where(core == 0, turned, packed).astype(BF)
    pair = (
        copy_to(kv_ref.at[core], kv_ref.at[core], pair_s.at[0], pair_r.at[0], (b, other(h, 1))),
        copy_to(
            bc_ref.at[:, :, pl.ds(pl.multiple_of(core * 128, 128), 128)],
            bc_ref.at[:, :, pl.ds(pl.multiple_of(core * 128, 128), 128)],
            pair_s.at[1], pair_r.at[1], (b, other(h, 1)),
        ),
    )
    for c in pair:
        c.start()
    line2.advance(0)
    dt = [pltpu.roll(kv[0], 128 - HDIM, 1), pltpu.roll(kv[1], 128 - HDIM + 8, 1)]
    dt_ref[...] = (
        jnp.where(lane < HG, dt[0], jnp.where((lane >= 8) & (lane < 8 + HG), dt[1], 0.0)).astype(BF).astype(F32)
    )
    for m in range(2):
        q = nn(normed_ref[m, LAG:], w1_ref[:, small + 128 : small + 256])
        q_ref[m] = rotate_pair(q, cos_ref[...], sin_ref[...]).astype(BF)
        xin_ref[m] = nn(normed_ref[m], w1_ref[:, XC : 2 * XC]).astype(BF)
        gate_ref[m] = nn(normed_ref[m, LAG:], w1_ref[:, :XC])
    for s in range(1, nb // 2 - 1):
        line2.advance(s)
    line2.finish()
    for c in pair:
        c.wait()
    gather_c.finish()
    for c in sent:
        c.wait_send()


def vm(shape, dtype):
    return jax.ShapeDtypeStruct(shape, dtype)


def call(kernel, outs, scratch, args, name, cid, smem=(), hbm=(), hbm_out=(), **cost):
    in_specs = [
        pl.BlockSpec(memory_space=pltpu.SMEM if i in smem else (pl.ANY if i in hbm else pltpu.VMEM))
        for i in range(len(args))
    ]
    out_specs = [
        pl.BlockSpec(memory_space=pl.ANY if i in hbm_out else pltpu.VMEM) for i in range(len(outs))
    ]
    return pl.pallas_call(
        kernel,
        out_shape=outs,
        in_specs=in_specs,
        out_specs=out_specs,
        scratch_shapes=scratch,
        compiler_params=pltpu.CompilerParams(
            collective_id=cid, has_side_effects=True, vmem_limit_bytes=VMEM_LIMIT
        ),
        name=name,
    )(*args)


def front(nb, x, cot, w1p, wrp, freq, local_pieces):
    tok = x.shape[1]
    T = tok * NH
    dma = pltpu.SemaphoreType.DMA
    outs = [
        vm((2, LAG + T, D), BF), vm((2, T, XC), F32), vm((2, LAG + T, XC), BF), vm((2, LAG + T, 256), BF),
        vm((2, T, 128), BF), vm((2, T, 128), BF), vm((T, 128), F32), vm((2, T, D), BF),
        vm((D, W1C), BF), vm((D, WRC), BF), vm((8, D), F32), vm((T, 128), F32), vm((T, 128), F32),
    ]
    scratch = (
        [pltpu.VMEM((2, LAG + T, D), BF)]
        + HeadGather.scratch() + HeadGather.scratch()
        + [dma((6,)), dma((6,))]
        + LineGather.scratch(nb) + LineGather.scratch(nb)
        + [dma((NH,)), dma((1,)), dma((1,)), dma((2,)), dma((2,))]
    )
    return call(
        functools.partial(front_kernel, nb, T, local_pieces), outs, scratch, (x, cot, w1p, wrp, freq), "front", 1,
    )


def doc_start(starts_ref, m, pos):
    first = jnp.zeros(pos.shape, jnp.int32)
    for k in range(starts_ref.shape[1]):
        s = starts_ref[m, k]
        first = jnp.where(pos >= s, s, first)
    return first


def head_row(ref, h, count=2):
    lane = lanes((1, 128))
    row = jnp.zeros((1, 128), F32)
    for i in range(HG):
        for m in range(count):
            row = jnp.where(lane == 8 * m + i, ref[h * HG + i], row)
    return row


def wide_row(ref, h):
    lane = lanes((1, XC)) // MHDIM
    row = jnp.zeros((1, XC), F32)
    for i in range(HG):
        row = jnp.where(lane == i, ref[h * HG + i], row)
    return row


def valid_row():
    lane = lanes((1, 128))
    return (lane < 16) & (lax.rem(lane, 8) < HG)


def triangle(n, upper=False):
    r, c = rows_of((n, n)), lanes((n, n))
    return ((c >= r) if upper else (c <= r)).astype(F32)


class Scan:
    ROWS = XC + 16

    def __init__(self, way, b, h, nb, reach, bufs):
        self.way, self.b, self.h, self.nb = way, b, h, nb
        self.steps = Scan.step_list(reach)
        self.send_buf, self.recv_buf, self.sums, self.send, self.recv = bufs

    @staticmethod
    def step_list(reach):
        steps, d = [], 1
        while d < reach:
            steps.append(d)
            d *= 2
        return steps + [1]

    @staticmethod
    def scratch(reach):
        n = len(Scan.step_list(reach))
        return [
            pltpu.VMEM((n, 2, Scan.ROWS, 128), BF),
            pltpu.VMEM((n, 2, Scan.ROWS, 128), BF),
            pltpu.VMEM((2, Scan.ROWS, 128), F32),
            pltpu.SemaphoreType.DMA((n,)),
            pltpu.SemaphoreType.DMA((n,)),
        ]

    @staticmethod
    def edges(b, h, nb, reach):
        out = []
        for d in sorted(set(Scan.step_list(reach))):
            out += [(b + d < nb, (b + d, h)), (b >= d, (b - d, h))]
        return out

    def has_to(self, d):
        return (self.b + d < self.nb) if self.way > 0 else (self.b >= d)

    def has_from(self, d):
        return (self.b >= d) if self.way > 0 else (self.b + d < self.nb)

    def copy(self, i):
        return copy_to(
            self.send_buf.at[i], self.recv_buf.at[i], self.send.at[i], self.recv.at[i],
            (self.b + self.way * self.steps[i], self.h),
        )

    def send_step(self, i):
        self.send_buf[i] = self.sums[...].astype(BF)

        @pl.when(self.has_to(self.steps[i]))
        def _():
            self.copy(i).start()

    def receive(self, i):
        there = self.has_from(self.steps[i])

        @pl.when(there)
        def _():
            self.copy(i).wait_recv()

        @pl.when(jnp.logical_not(there))
        def _():
            self.recv_buf[i] = jnp.zeros((2, Scan.ROWS, 128), BF)

    def join(self, i):
        self.receive(i)
        for m in range(2):
            early = self.recv_buf[i, m].astype(F32)
            for j in range(HG):
                mine = pl.ds(j * MHDIM, MHDIM)
                decay = self.sums[m, pl.ds(XC + j, 1), :]
                self.sums[m, mine, :] = self.sums[m, mine, :] + decay * early[j * MHDIM : (j + 1) * MHDIM]
            self.sums[m, pl.ds(XC, 8), :] = self.sums[m, pl.ds(XC, 8), :] * early[XC : XC + 8]

    def finish(self):
        for i, d in enumerate(self.steps):

            @pl.when(self.has_to(d))
            def _():
                self.copy(i).wait_send()


def halo_edges(b, h, nb, reach):
    out = []
    for d in range(1, reach + 1):
        out += [(b + d < nb, (b + d, h)), (b >= d, (b - d, h))]
    return out


class Halo:
    def __init__(self, way, src, dst, b, h, nb, reach, sems):
        self.way, self.src, self.dst, self.b, self.h, self.nb, self.reach = way, src, dst, b, h, nb, reach
        self.send, self.recv = sems

    @staticmethod
    def scratch(reach):
        return [pltpu.SemaphoreType.DMA((reach + 1,))] * 2

    def there(self, d, way):
        return (self.b + d < self.nb) if way > 0 else (self.b >= d)

    def copy(self, d):
        return copy_to(
            self.src(d), self.dst(d), self.send.at[d], self.recv.at[d], (self.b + self.way * d, self.h)
        )

    def begin(self):
        for d in range(1, self.reach + 1):

            @pl.when(self.there(d, self.way))
            def _():
                self.copy(d).start()

    def finish_recv(self):
        for d in range(1, self.reach + 1):

            @pl.when(self.there(d, -self.way))
            def _():
                self.copy(d).wait_recv()

    def finish_send(self):
        for d in range(1, self.reach + 1):

            @pl.when(self.there(d, self.way))
            def _():
                self.copy(d).wait_send()


class HeadSum:
    def __init__(self, b, h, bufs):
        self.b, self.h = b, h
        self.buf, self.send, self.recv = bufs

    @staticmethod
    def scratch(T):
        return [pltpu.VMEM((4, 8, T), F32), pltpu.SemaphoreType.DMA((3,)), pltpu.SemaphoreType.DMA((3,))]

    def copies(self):
        return [
            copy_to(self.buf.at[0], self.buf.at[1 + i], self.send.at[i], self.recv.at[i], (self.b, to))
            for i, to in enumerate((other(self.h, 1), other(self.h, 2), NH - 1 - self.h))
        ]

    def begin(self, cols):
        T = self.buf.shape[2]
        lane = lanes((T, 128))
        packed = jnp.where(lane == 0, cols[0], jnp.where(lane == 1, cols[1], 0.0))
        self.buf[0] = packed.T[:8]
        for c in self.copies():
            c.start()

    def finish(self):
        for c in self.copies():
            c.wait()
        T = self.buf.shape[2]
        total = self.buf[0] + self.buf[1] + self.buf[2] + self.buf[3]
        cols = jnp.concatenate([total, jnp.zeros((120, T), F32)], axis=0).T
        return [cols[:, 0:1], cols[:, 1:2]]


def group_taps(h, w_ref, b_ref, chunk):
    if chunk < XC // 128:
        at = pl.ds(pl.multiple_of(h * XC + chunk * 128, 128), 128)
    else:
        at = pl.ds(DI + (chunk - XC // 128) * 128, 128)
    return w_ref[:, at], b_ref[:, at]


def decays_of(dt_ref, bias_ref, alog_ref, h, T):
    valid = valid_row()
    z = dt_ref[...] + head_row(bias_ref, h)
    step = jnp.where(valid, jnp.maximum(z, 0.0) + jnp.log1p(jnp.exp(-jnp.abs(z))), 0.0)
    a_neg = jnp.where(valid, -jnp.exp(head_row(alog_ref, h)), 0.0)
    cum = jnp.dot(triangle(T), step * a_neg, precision=high, preferred_element_type=F32)
    return z, step, a_neg, cum


def by_batch(pick):
    first, second = pick(0), pick(1)
    return jnp.where(lanes((first.shape[0], 128)) < 8, first, second)


def mixer_kernel(
    nb, T, reach,
    xin_ref, bc_ref, q_ref, kv_ref, dt_ref, gate_ref, starts_ref, cw_ref, cb_ref, dtb_ref, alog_ref, skip_ref, gain_ref,
    ylow_ref, gated_ref, attnf_ref, attnl_ref, r_ref, lse_ref, pre_ref, sin_ref, kvh_ref,
    cin, xs, bs, cs, ybuf, sbuf, cumt, stept, c0, c1, c2, c3, c4, h0, h1, t0, t1, t2,
):
    b, h = place()
    barrier(head_edges(b, h) + Scan.edges(b, h, nb, reach) + halo_edges(b, h, nb, reach))
    scan = Scan(1, b, h, nb, reach, (c0, c1, c2, c3, c4))
    halo = Halo(1, lambda d: kv_ref, lambda d: kvh_ref.at[d], b, h, nb, reach, (h0, h1))
    sums = HeadSum(b, h, (t0, t1, t2))
    halo.begin()
    pos = b * T + rows_of((T, 1))
    first = [doc_start(starts_ref, m, pos) for m in range(2)]
    last = [f[T - 1 :, :] for f in first]
    for d in range(1, reach + 1):

        @pl.when(b < d)
        def _():
            kvh_ref[d] = jnp.zeros((2, T, 128), BF)

    kvh_ref[0] = kv_ref[...]
    for m in range(2):
        cin[:, 0:XC] = xin_ref[m].astype(F32)
        cin[:, XC:] = bc_ref[m].astype(F32)
        for chunk in range((XC + 256) // 128):
            cols = pl.ds(chunk * 128, 128)
            taps, bias = group_taps(h, cw_ref, cb_ref, chunk)
            total = jnp.broadcast_to(bias, (T, 128))
            for j in range(4):
                back = 3 - j
                total = total + jnp.where(pos - first[m] >= back, cin[pl.ds(LAG - back, T), cols] * taps[j : j + 1], 0.0)
            pre_ref[m, :, cols] = total
            act = total * sigmoid(total)
            if chunk < XC // 128:
                xs[m, :, cols] = act
            elif chunk == XC // 128:
                bs[m] = act.astype(BF)
            else:
                cs[m] = act.astype(BF)
    z, step, a_neg, cum = decays_of(dt_ref, dtb_ref, alog_ref, h, T)
    cumt[...] = cum.T[:16]
    stept[...] = step.T[:16]
    cum_last = cum[T - 1 :, :]
    kept = by_batch(lambda m: jnp.broadcast_to((pos >= last[m]).astype(F32), (T, 128)))
    omega = jnp.exp(cum_last - cum) * step * kept
    for m in range(2):
        weighted = (xs[m] * widen(omega, 8 * m)).astype(BF)
        scan.sums[m, 0:XC, :] = tn(weighted, bs[m])
        decay = jnp.where(last[m] < b * T, jnp.exp(cumt[8 * m : 8 * m + 8, T - 1 : T]), 0.0)
        scan.sums[m, XC : XC + 8, :] = jnp.broadcast_to(decay, (8, 128))
        scan.sums[m, XC + 8 :, :] = jnp.zeros((8, 128), F32)
    scan.send_step(0)

    seen = lanes((T, T)) + b * T
    for m in range(2):
        both = nt(cs[m], bs[m])
        allowed = (seen <= pos) & (seen >= first[m])
        for i in range(HG):
            l = 8 * m + i
            gap = jnp.where(allowed, cum[:, l : l + 1] - cumt[l : l + 1, :], FAR)
            weights = (jnp.exp(gap) * both * stept[l : l + 1, :]).astype(BF)
            ybuf[m, :, i * MHDIM : (i + 1) * MHDIM] = nn(weights, xs[m, :, i * MHDIM : (i + 1) * MHDIM].astype(BF))
        ybuf[m] = ybuf[m] + wide_row(skip_ref, h) * xs[m]
        if m == 0:
            scan.join(0)
            scan.send_step(1)
    halo.finish_recv()

    lane = lanes((T, 128))
    lse_all = jnp.zeros((T, 128), F32)
    for m in range(2):
        for i in range(2):
            query = q_ref[m, :, i * HDIM : (i + 1) * HDIM]

            def score(d, top):
                at = seen - d * T
                keys = kvh_ref[d, 0, :, m * HDIM : (m + 1) * HDIM]
                s = jnp.where((at <= pos) & (at >= first[m]), nt(query, keys) * SCALE, FAR)
                sbuf[d] = s
                return jnp.maximum(top, jnp.max(s, axis=1, keepdims=True))

            top = lax.fori_loop(0, reach + 1, score, jnp.full((T, 1), FAR, F32))

            def weigh(d, total):
                e = jnp.exp(sbuf[d] - top)
                sbuf[d] = e
                return total + jnp.sum(e, axis=1, keepdims=True)

            total = lax.fori_loop(0, reach + 1, weigh, jnp.zeros((T, 1), F32))
            inverse = 1.0 / total

            def take(d, acc):
                probs = (sbuf[d] * inverse).astype(BF)
                return acc + nn(probs, kvh_ref[d, 1, :, m * HDIM : (m + 1) * HDIM])

            attnf_ref[m, :, i * HDIM : (i + 1) * HDIM] = lax.fori_loop(0, reach + 1, take, jnp.zeros((T, HDIM), F32))
            lse_all = jnp.where(lane == 2 * m + i, top + jnp.log(total), lse_all)
        attnl_ref[m] = attnf_ref[m].astype(BF)
        if len(scan.steps) > 2 and m == 0:
            scan.join(1)
            scan.send_step(2)
    lse_ref[...] = lse_all
    for i in range(2, len(scan.steps) - 1):
        scan.join(i)
        scan.send_step(i + 1)
    end = len(scan.steps) - 1
    scan.receive(end)
    sin_ref[...] = c1[end]
    squares = []
    for m in range(2):
        live = jnp.where(first[m] < b * T, jnp.exp(cum), 0.0)
        y = ybuf[m] + nt(cs[m], sin_ref[m, 0:XC]) * widen(live, 8 * m)
        low = y.astype(BF)
        ylow_ref[m] = low
        gate = gate_ref[m]
        g = low.astype(F32) * gate * sigmoid(gate)
        ybuf[m] = g
        squares.append(jnp.sum(g * g, axis=1, keepdims=True))
    sums.begin(squares)
    scan.finish()
    halo.finish_send()
    gain = gain_ref[:, pl.ds(pl.multiple_of(h * XC, 128), XC)]
    totals = sums.finish()
    scales = [lax.rsqrt(t * (1.0 / DI) + EPS) for t in totals]
    for m in range(2):
        gated_ref[m] = (ybuf[m] * scales[m] * gain).astype(BF)
    r_ref[...] = jnp.where(lane == 0, scales[0], jnp.where(lane == 1, scales[1], 0.0))


def mixer(nb, reach, xin, bc, q, kv, dt, gate, starts, cw, cb, dtb, alog, skip, gain):
    T = q.shape[1]
    outs = [
        vm((2, T, XC), BF), vm((2, T, XC), BF), vm((2, T, 128), F32), vm((2, T, 128), BF), vm((T, 128), F32),
        vm((T, 128), F32), vm((2, T, XC + 256), F32), vm((2, Scan.ROWS, 128), BF), vm((reach + 1, 2, T, 128), BF),
    ]
    scratch = (
        [
            pltpu.VMEM((LAG + T, XC + 256), F32), pltpu.VMEM((2, T, XC), F32), pltpu.VMEM((2, T, 128), BF),
            pltpu.VMEM((2, T, 128), BF), pltpu.VMEM((2, T, XC), F32), pltpu.VMEM((reach + 1, T, T), F32),
            pltpu.VMEM((16, T), F32), pltpu.VMEM((16, T), F32),
        ]
        + Scan.scratch(reach) + Halo.scratch(reach) + HeadSum.scratch(T)
    )
    return call(
        functools.partial(mixer_kernel, nb, T, reach), outs, scratch,
        (xin, bc, q, kv, dt, gate, starts, cw, cb, dtb, alog, skip, gain), "mixer", 2, smem=(6, 9, 10, 11),
    )


def norm_back(value, scale, gain, upstream):
    n = value * scale
    uw = upstream * gain
    grad = scale * (uw - n * jnp.mean(n * uw, axis=1, keepdims=True))
    return grad, jnp.sum(upstream * n, axis=0, keepdims=True)


def arrange(per, width, first):
    total = XC + 128
    share, mix, att = total // per, XC // per, 128 // per
    n, src = lanes((width, total)), rows_of((width, total))
    i, u = n // share, lax.rem(n, share)
    if first == 0:
        hit = (u < mix) & (src == i * mix + u)
    else:
        hit = (u >= mix) & (src == i * att + u - mix)
    return hit.astype(F32).astype(BF)


def feed_kernel(
    nb, T,
    gated_ref, attnl_ref, x_ref, cot_ref, cotg_ref, wr_ref, gains_ref, ylow_ref, gate_ref, r_ref, gain_ref,
    out_ref, gh_ref, gy_ref, ggate_ref, gattn_ref, gwr_ref, gn2_ref, ggain_ref,
    part, part2, secg, hlg, act, ggu, gact, hid, w0, w1, w2, w3, w4, w5, v0, v1, v2, v3, v4, v5, u0, u1, u2, u3, u4, u5,
    a0, a1, b0, b1, t0, t1, t2,
):
    b, h = place()
    tok = T // NH
    barrier(head_edges(b, h))
    n2 = gains_ref[7:8, :]

    def rows(ref):
        return lambda m, head: ref[m, pl.ds(pl.multiple_of(head * tok, tok), tok), :]

    at_gate, at_mix, at_att, at_out = 0, 2 * FG, 2 * FG + XC, 2 * FG + XC + 128
    for m in range(2):
        part[m] = nt(gated_ref[m], wr_ref[:, at_mix:at_att]) + nt(attnl_ref[m], wr_ref[:, at_att:at_out])
    first = HeadScatter(rows(part), b, h, (w0, w1, w2, w3), (w4, w5))
    first.begin()
    gact[0] = nn(cotg_ref[0], wr_ref[:, at_out:])
    first.middle()
    gact[1] = nn(cotg_ref[1], wr_ref[:, at_out:])
    first.finish()
    gather_s = HeadGather(lambda i: secg.at[:, pl.ds(i * tok, tok)], b, h, (a0, a1))
    for m in range(2):
        value = x_ref[m].astype(F32) + first.result(m)
        hid[m] = value
        scale = lax.rsqrt(jnp.mean(value * value, axis=1, keepdims=True) + EPS)
        secg[m, pl.ds(pl.multiple_of(h * tok, tok), tok), :] = (value * scale * n2).astype(BF)
    gather_s.begin()
    gather_s.forward()
    gather_s.finish()
    for m in range(2):
        a = nn(secg[m], wr_ref[:, 0:FG])
        u = nn(secg[m], wr_ref[:, FG : 2 * FG])
        sg = sigmoid(a)
        si = a * sg
        act[m] = (si * u).astype(BF)
        ggu[m, :, 0:FG] = (gact[m] * u * (sg * (1.0 + a * (1.0 - sg)))).astype(BF)
        ggu[m, :, FG:] = (gact[m] * si).astype(BF)
    for m in range(2):
        part[m] = nt(ggu[m], wr_ref[:, 0 : 2 * FG])
    second = HeadScatter(rows(part), b, h, (v0, v1, v2, v3), (v4, v5))
    second.begin()
    part2[0] = nt(act[0], wr_ref[:, at_out:])
    second.middle()
    part2[1] = nt(act[1], wr_ref[:, at_out:])
    second.finish()
    third = HeadScatter(rows(part2), b, h, (u0, u1, u2, u3), (u4, u5))
    gather_h = HeadGather(lambda i: hlg.at[:, pl.ds(i * tok, tok)], b, h, (b0, b1))
    gn2 = jnp.zeros((1, D), F32)
    for m in range(2):
        value = hid[m]
        scale = lax.rsqrt(jnp.mean(value * value, axis=1, keepdims=True) + EPS)
        grad, gain_part = norm_back(value, scale, n2, second.result(m))
        grad = grad + cot_ref[m].astype(F32)
        gh_ref[m] = grad
        gn2 = gn2 + gain_part
        hlg[m, pl.ds(pl.multiple_of(h * tok, tok), tok), :] = grad.astype(BF)
    gn2_ref[...] = gn2
    gather_h.begin()
    third.begin()

    def both(ref, cols):
        return [ref[m, :, cols] for m in range(2)]

    for k in range(4):
        cols = slice(k * FG // 2, (k + 1) * FG // 2)
        gwr_ref[:, cols] = sum(tn(secg[m], ggu[m, :, cols]) for m in range(2)).astype(BF)
        if k == 0:
            gather_h.forward()
        if k == 1:
            third.middle()
    for k in range(2):
        cols = slice(k * FG // 2, (k + 1) * FG // 2)
        gwr_ref[:, at_out + cols.start : at_out + cols.stop] = sum(
            tn(cotg_ref[m], act[m, :, cols]) for m in range(2)
        ).astype(BF)
    gather_h.finish()
    sums = HeadSum(b, h, (t0, t1, t2))
    gain = gain_ref[:, pl.ds(pl.multiple_of(h * XC, 128), XC)]
    dots = []
    ggain = jnp.zeros((1, XC), F32)
    for m in range(2):
        part[m, :, 0:XC] = nn(hlg[m], wr_ref[:, at_mix:at_att])
        gattn_ref[m] = nn(hlg[m], wr_ref[:, at_att:at_out]).astype(BF)
        gate = gate_ref[m]
        si = gate * sigmoid(gate)
        n = ylow_ref[m].astype(F32) * si * r_ref[:, m : m + 1]
        up = part[m, :, 0:XC]
        ggain = ggain + jnp.sum(up * n, axis=0, keepdims=True)
        dots.append(jnp.sum(up * gain * n, axis=1, keepdims=True))
    ggain_ref[...] = ggain
    sums.begin(dots)
    third.finish()
    for m in range(2):
        out_ref[m] = hid[m] + third.result(m)
    per = max(nb // NH, 1)
    mix_to, att_to = arrange(per, XC, 0), arrange(per, 128, 1)
    for m in range(2):
        act[m] = (nn(gated_ref[m], mix_to) + nn(attnl_ref[m], att_to)).astype(BF)
    for k in range(2):
        cols = slice(k * FG // 2, (k + 1) * FG // 2)
        gwr_ref[:, at_mix + cols.start : at_mix + cols.stop] = sum(tn(hlg[m], act[m, :, cols]) for m in range(2)).astype(BF)
    totals = sums.finish()
    for m in range(2):
        gate = gate_ref[m]
        sg = sigmoid(gate)
        si = gate * sg
        low = ylow_ref[m].astype(F32)
        scale = r_ref[:, m : m + 1]
        n = low * si * scale
        grad = scale * (part[m, :, 0:XC] * gain - n * (totals[m] * (1.0 / DI)))
        gy_ref[m] = (grad * si).astype(BF)
        ggate_ref[m] = (grad * low * (sg * (1.0 + gate * (1.0 - sg)))).astype(BF)


def feed(nb, gated, attnl, x, cot, cotg, wr, gains, ylow, gate, r, gain):
    T = gated.shape[1]
    tok = T // NH
    outs = [
        vm((2, tok, D), F32), vm((2, tok, D), F32), vm((2, T, XC), BF), vm((2, T, XC), BF), vm((2, T, 128), BF),
        vm((D, WRC), BF), vm((1, D), F32), vm((1, XC), F32),
    ]
    scratch = (
        [
            pltpu.VMEM((2, T, D), F32), pltpu.VMEM((2, T, D), F32), pltpu.VMEM((2, T, D), BF), pltpu.VMEM((2, T, D), BF),
            pltpu.VMEM((2, T, FG), BF), pltpu.VMEM((2, T, 2 * FG), BF), pltpu.VMEM((2, T, FG), F32),
            pltpu.VMEM((2, tok, D), F32),
        ]
        + HeadScatter.scratch(tok) * 3 + HeadGather.scratch() * 2 + HeadSum.scratch(T)
    )
    return call(
        functools.partial(feed_kernel, nb, T), outs, scratch,
        (gated, attnl, x, cot, cotg, wr, gains, ylow, gate, r, gain), "feed", 3,
    )


def head_select(m):
    return (lanes((XC, 128)) == 8 * m + rows_of((XC, 128)) // MHDIM).astype(F32)


def exact(a, b):
    return jnp.dot(a, b, precision=high, preferred_element_type=F32)


def back_kernel(
    nb, T, reach,
    gy_ref, gattn_ref, q_ref, kvh_ref, attnf_ref, lse_ref, pre_ref, xin_ref, bc_ref, dt_ref, sin_ref, ggate_ref,
    starts_ref, cw_ref, cb_ref, dtb_ref, alog_ref, skip_ref, cos_ref, sine_ref, normed_ref, w1_ref, x_ref, gh_ref, gains_ref,
    gin_ref, gw1_ref, gcw_ref, gsmall_ref, gn1_ref,
    cin, xs, bs, cs, cumt, stept, gx, gbm, gcm, gcin, gq, gkv, gkvs, gkvr, gproj, gnp, rowq,
    pair_b, pair_k, pair_kr, pair_r, yb_s, yb_r, edge_s, edge_r,
    c0, c1, c2, c3, c4, h0, h1, w0, w1, w2, w3, w4, w5, es, er, ps, pr,
):
    b, h = place()
    tok = T // NH
    core, y = lax.rem(h, 2), h // 2
    barrier(
        head_edges(b, h) + Scan.edges(b, h, nb, reach) + halo_edges(b, h, nb, reach)
        + [((h == NH - 1) & (b + 1 < nb), (b + 1, jnp.int32(i))) for i in range(NH)]
        + [(b >= 1, (b - 1, jnp.int32(NH - 1)))]
    )
    scan = Scan(-1, b, h, nb, reach, (c0, c1, c2, c3, c4))
    halo = Halo(-1, lambda d: gkvs.at[d], lambda d: gkvr.at[d], b, h, nb, reach, (h0, h1))
    pos = b * T + rows_of((T, 1))
    first = [doc_start(starts_ref, m, pos) for m in range(2)]
    last = [f[T - 1 :, :] for f in first]
    seen = lanes((T, T)) + b * T
    lane = lanes((T, 128))
    for m in range(2):
        for chunk in range((XC + 256) // 128):
            cols = pl.ds(chunk * 128, 128)
            total = pre_ref[m, :, cols]
            act = total * sigmoid(total)
            if chunk < XC // 128:
                xs[m, :, cols] = act
            elif chunk == XC // 128:
                bs[m] = act.astype(BF)
            else:
                cs[m] = act.astype(BF)
    z, step, a_neg, cum = decays_of(dt_ref, dtb_ref, alog_ref, h, T)
    cumt[...] = cum.T[:16]
    stept[...] = step.T[:16]
    cum_last = cum[T - 1 :, :]
    live = jnp.exp(cum) * by_batch(lambda m: jnp.broadcast_to((first[m] < b * T).astype(F32), (T, 128)))
    kept = jnp.exp(cum_last - cum) * by_batch(lambda m: jnp.broadcast_to((pos >= last[m]).astype(F32), (T, 128)))
    omega = kept * step
    for m in range(2):
        u = (gy_ref[m].astype(F32) * widen(live, 8 * m)).astype(BF)
        scan.sums[m, 0:XC, :] = tn(u, cs[m])
        decay = jnp.where(last[m] < b * T, jnp.exp(cumt[8 * m : 8 * m + 8, T - 1 : T]), 0.0)
        scan.sums[m, XC : XC + 8, :] = jnp.broadcast_to(decay, (8, 128))
        scan.sums[m, XC + 8 :, :] = jnp.zeros((8, 128), F32)
    scan.send_step(0)

    gkv[...] = jnp.zeros_like(gkv)
    for m in range(2):
        for i in range(2):
            mine = slice(i * HDIM, (i + 1) * HDIM)
            query, grad = q_ref[m, :, mine], gattn_ref[m, :, mine]
            delta = jnp.sum(grad.astype(F32) * attnf_ref[m, :, mine], axis=1, keepdims=True)
            lse = lse_ref[:, 2 * m + i : 2 * m + i + 1]

            def block(d, acc):
                at = seen - d * T
                keys = kvh_ref[d, 0, :, m * HDIM : (m + 1) * HDIM]
                vals = kvh_ref[d, 1, :, m * HDIM : (m + 1) * HDIM]
                probs = jnp.where((at <= pos) & (at >= first[m]), jnp.exp(nt(query, keys) * SCALE - lse), 0.0)
                ds = (probs * (nt(grad, vals) - delta)).astype(BF)
                gkv[d, 0, :, m * HDIM : (m + 1) * HDIM] += tn(ds, query) * SCALE
                gkv[d, 1, :, m * HDIM : (m + 1) * HDIM] += tn(probs.astype(BF), grad)
                return acc + nn(ds, keys)

            gq[m, :, mine] = lax.fori_loop(0, reach + 1, block, jnp.zeros((T, HDIM), F32)) * SCALE
    gkvs[...] = gkv[...].astype(BF)
    halo.begin()
    scan.join(0)
    scan.send_step(1)

    row_sums = jnp.zeros((T, 128), F32)
    rowq[...] = jnp.zeros_like(rowq)
    skip = wide_row(skip_ref, h)
    gskip = jnp.zeros((1, 128), F32)
    for m in range(2):
        both = nt(cs[m], bs[m])
        allowed = (seen <= pos) & (seen >= first[m])
        gboth = jnp.zeros((T, T), F32)
        for i in range(HG):
            l = 8 * m + i
            mine = slice(i * MHDIM, (i + 1) * MHDIM)
            grad = gy_ref[m, :, mine]
            decay = jnp.exp(jnp.where(allowed, cum[:, l : l + 1] - cumt[l : l + 1, :], FAR))
            srow = stept[l : l + 1, :]
            ld = decay * nt(grad, xs[m, :, mine].astype(BF))
            gboth = gboth + ld * srow
            q = ld * both
            rowq[l : l + 1, :] = jnp.sum(q, axis=0, keepdims=True)
            row_sums = jnp.where(lane == l, jnp.sum(q * srow, axis=1, keepdims=True), row_sums)
            gx[m, :, mine] = tn((decay * both * srow).astype(BF), grad)
        low = gboth.astype(BF)
        gcm[m] = nn(low, bs[m])
        gbm[m] = tn(low, cs[m])
        gyf = gy_ref[m].astype(F32)
        gskip = gskip + exact(jnp.sum(gyf * xs[m], axis=0, keepdims=True), head_select(m))
        gx[m] = gx[m] + skip * gyf
        u = gyf * widen(live, 8 * m)
        carried = nt(cs[m], sin_ref[m, 0:XC])
        row_sums = row_sums + exact(u * carried, head_select(m))
        gcm[m] += nn(u.astype(BF), sin_ref[m, 0:XC])
        if m == 0 and len(scan.steps) > 2:
            scan.join(1)
            scan.send_step(2)
    for i in range(2, len(scan.steps) - 1):
        scan.join(i)
        scan.send_step(i + 1)

    halo.finish_recv()
    for k in range(2):
        total = gkv[0, k]
        for d in range(1, reach + 1):
            total = total + jnp.where(b + d < nb, gkvr[d, k].astype(F32), 0.0)
        gkv[0, k] = total
    pair_k[...] = gkv[0, 1 - core].astype(BF)
    swap_k = copy_to(pair_k, pair_kr, ps.at[0], pr.at[0], (b, other(h, 1)))
    swap_k.start()

    end = len(scan.steps) - 1
    scan.receive(end)
    colq = jnp.concatenate([rowq[...], jnp.zeros((112, T), F32)], axis=0).T
    gstep = colq
    gcum = row_sums - step * colq
    glast = jnp.zeros((1, 128), F32)
    for m in range(2):
        adjoint = c1[end, m, 0:XC]
        read = nt(bs[m], adjoint)
        wide = widen(omega, 8 * m)
        gx[m] += wide * read
        gbm[m] += nn((xs[m] * wide).astype(BF), adjoint)
        gw = exact(xs[m] * read, head_select(m))
        gstep = gstep + kept * gw
        term = omega * gw
        gcum = gcum - term
        glast = glast + jnp.sum(term, axis=0, keepdims=True)
        through = jnp.where(last[m] < b * T, jnp.exp(cum_last), 0.0)
        overlap = adjoint.astype(F32) * sin_ref[m, 0:XC].astype(F32)
        per_head = jnp.sum(
            lax.dot_general(overlap, head_select(m), (((0,), (0,)), ((), ())), precision=high, preferred_element_type=F32),
            axis=0, keepdims=True,
        )
        glast = glast + through * per_head
    gcum = gcum + jnp.where(rows_of((T, 128)) == T - 1, glast, 0.0)
    gda = exact(triangle(T, upper=True), gcum)
    gstep = gstep + gda * a_neg
    gz = jnp.where(valid_row(), gstep * sigmoid(z), 0.0)
    small = jnp.concatenate(
        [
            jnp.sum(gz, axis=0, keepdims=True),
            jnp.sum(gda * step, axis=0, keepdims=True) * a_neg,
            gskip,
            jnp.zeros((5, 128), F32),
        ],
        axis=0,
    )
    gsmall_ref[...] = small + pltpu.roll(small, 120, 1)

    gcw_ref[...] = jnp.zeros_like(gcw_ref)
    gcin[...] = jnp.zeros_like(gcin)
    for m in range(2):
        cin[:, 0:XC] = xin_ref[m].astype(F32)
        cin[:, XC:] = bc_ref[m].astype(F32)
        for chunk in range((XC + 256) // 128):
            cols = pl.ds(chunk * 128, 128)
            taps, _ = group_taps(h, cw_ref, cb_ref, chunk)
            pre = pre_ref[m, :, cols]
            sg = sigmoid(pre)
            if chunk < XC // 128:
                up = gx[m, :, cols]
            elif chunk == XC // 128:
                up = gbm[m]
            else:
                up = gcm[m]
            gs = up * (sg * (1.0 + pre * (1.0 - sg)))
            gcw_ref[4:5, cols] += jnp.sum(gs, axis=0, keepdims=True)
            for back in range(4):
                j = 3 - back
                kept_gs = jnp.where(pos - first[m] >= back, gs, 0.0)
                gcw_ref[j : j + 1, cols] += jnp.sum(
                    jnp.where(pos - first[m] >= back, gs * cin[pl.ds(LAG - back, T), cols], 0.0), axis=0, keepdims=True
                )
                gcin[m, pl.ds(LAG - back, T), cols] += kept_gs * taps[j : j + 1]

    for m in range(2):
        pair_b[m] = gcin[m, :, pl.ds(pl.multiple_of(XC + (1 - core) * 128, 128), 128)].astype(BF)
    swap_b = copy_to(pair_b, pair_r, ps.at[1], pr.at[1], (b, other(h, 1)))
    swap_b.start()
    swap_k.wait()
    packed = gkv[0, core] + pair_kr[...].astype(F32)
    turned = rotate_pair(packed, cos_ref[...], -sine_ref[...])
    packed = jnp.where(core == 0, turned, packed)
    for m in range(2):
        gproj[m, 0:LAG, 0:XC] = jnp.zeros((LAG, XC), BF)
        gproj[m, LAG:, 0:XC] = ggate_ref[m]
        gproj[m, :, XC : 2 * XC] = gcin[m, :, 0:XC].astype(BF)
        gproj[m, 0:LAG, 2 * XC + 128 :] = jnp.zeros((LAG, 256), BF)
        gproj[m, LAG:, 2 * XC + 128 : 2 * XC + 256] = rotate_pair(gq[m], cos_ref[...], -sine_ref[...]).astype(BF)
        mine = packed if m == 0 else pltpu.roll(packed, HDIM, 1)
        gdt = pltpu.roll(gz, HDIM - 8 * m, 1)
        gproj[m, LAG:, 2 * XC + 256 :] = jnp.where(
            lane < HDIM, mine, jnp.where(lane < HDIM + HG, gdt, 0.0)
        ).astype(BF)
    swap_b.wait()
    for m in range(2):
        total = gcin[m, :, pl.ds(pl.multiple_of(XC + core * 128, 128), 128)] + pair_r[m].astype(F32)
        gcin[m, :, 0:128] = total
        yb_s[m] = total.astype(BF)
    swap_y = copy_to(yb_s, yb_r, ps.at[2], pr.at[2], (b, other(h, 2)))
    swap_y.start()
    swap_y.wait()
    half = lanes((LAG + T, 128)) // HDIM == y
    for m in range(2):
        total = gcin[m, :, 0:128] + yb_r[m].astype(F32)
        gproj[m, :, 2 * XC : 2 * XC + 128] = jnp.where(half, total, 0.0).astype(BF)

    for m in range(2):
        gnp[m] = nt(gproj[m], w1_ref[...])
    scatter = HeadScatter(
        lambda m, head: gnp[m, pl.ds(pl.multiple_of(LAG + head * tok, LAG), tok), :], b, h, (w0, w1, w2, w3), (w4, w5)
    )
    scatter.begin()
    for m in range(2):
        edge_s[m] = gnp[m, 0:LAG, :].astype(BF)

    def edge(i):
        return copy_to(edge_s, edge_r.at[i], es.at[0], er.at[i], (b - 1, jnp.int32(NH - 1)))

    @pl.when(b >= 1)
    def _():
        edge(h).start()

    scatter.middle()
    third = W1C // 3
    for k in range(3):
        cols = slice(k * third, (k + 1) * third)
        gw1_ref[:, cols] = sum(tn(normed_ref[m], gproj[m, :, cols]) for m in range(2)).astype(BF)
    scatter.finish()

    @pl.when(b >= 1)
    def _():
        edge(h).wait_send()

    mine = (h == NH - 1) & (b + 1 < nb)

    @pl.when(mine)
    def _():
        for i in range(NH):
            edge(i).wait_recv()

    @pl.when(jnp.logical_not(mine))
    def _():
        edge_r[...] = jnp.zeros_like(edge_r)

    n1 = gains_ref[6:7, :]
    gn1 = jnp.zeros((1, D), F32)
    for m in range(2):
        gnp[m, 0:tok, :] = scatter.result(m)
        gnp[m, tok - LAG : tok, :] += sum(edge_r[i, m].astype(F32) for i in range(NH))
        value = x_ref[m].astype(F32)
        scale = lax.rsqrt(jnp.mean(value * value, axis=1, keepdims=True) + EPS)
        grad, part = norm_back(value, scale, n1, gnp[m, 0:tok, :])
        gn1 = gn1 + part
        gin_ref[m] = gh_ref[m] + grad
    gn1_ref[...] = gn1
    scan.finish()
    halo.finish_send()


def back(nb, reach, *args):
    gy, q = args[0], args[2]
    T = q.shape[1]
    tok = T // NH
    dma = pltpu.SemaphoreType.DMA
    outs = [vm((2, tok, D), F32), vm((D, W1C), BF), vm((8, XC + 256), F32), vm((8, 128), F32), vm((1, D), F32)]
    scratch = (
        [
            pltpu.VMEM((LAG + T, XC + 256), F32), pltpu.VMEM((2, T, XC), F32), pltpu.VMEM((2, T, 128), BF),
            pltpu.VMEM((2, T, 128), BF), pltpu.VMEM((16, T), F32), pltpu.VMEM((16, T), F32),
            pltpu.VMEM((2, T, XC), F32), pltpu.VMEM((2, T, 128), F32), pltpu.VMEM((2, T, 128), F32),
            pltpu.VMEM((2, LAG + T, XC + 256), F32), pltpu.VMEM((2, T, 128), F32),
            pltpu.VMEM((reach + 1, 2, T, 128), F32), pltpu.VMEM((reach + 1, 2, T, 128), BF),
            pltpu.VMEM((reach + 1, 2, T, 128), BF), pltpu.VMEM((2, LAG + T, W1C), BF),
            pltpu.VMEM((2, LAG + T, D), F32), pltpu.VMEM((16, T), F32),
            pltpu.VMEM((2, LAG + T, 128), BF), pltpu.VMEM((T, 128), BF), pltpu.VMEM((T, 128), BF),
            pltpu.VMEM((2, LAG + T, 128), BF),
            pltpu.VMEM((2, LAG + T, 128), BF), pltpu.VMEM((2, LAG + T, 128), BF),
            pltpu.VMEM((2, LAG, D), BF), pltpu.VMEM((NH, 2, LAG, D), BF),
        ]
        + Scan.scratch(reach) + Halo.scratch(reach) + HeadScatter.scratch(tok)
        + [dma((1,)), dma((NH,)), dma((3,)), dma((3,))]
    )
    return call(functools.partial(back_kernel, nb, T, reach), outs, scratch, args, "back", 4, smem=(12, 15, 16, 17))


class LineReduce:
    def __init__(self, src, bufs, b, h, nb):
        self.src, self.h, self.nz = src, h, nb // 2
        self.z, self.x = b // 2, lax.rem(b, 2)
        self.total, self.from_x, self.from_l, self.from_r, self.xs, self.xr, self.ls, self.lr, self.rs, self.rr = bufs
        order, low, top = [], 0, self.nz - 1
        while low <= top:
            order += [top] if low == top else [top, low]
            low, top = low + 1, top - 1
        self.order = order

    @staticmethod
    def scratch(nb, cols):
        nz, rpb = nb // 2, D // nb
        return [pltpu.VMEM((nz, rpb, cols), BF)] * 4 + [pltpu.SemaphoreType.DMA((nz,))] * 6

    def to_x(self, z):
        return copy_to(
            self.src.at[z, 1 - self.x], self.from_x.at[z], self.xs.at[z], self.xr.at[z], (2 * self.z + 1 - self.x, self.h)
        )

    def up(self, z):
        return copy_to(
            self.total.at[z], self.from_l.at[z], self.rs.at[z], self.lr.at[z], (2 * (self.z + 1) + self.x, self.h)
        )

    def down(self, z):
        return copy_to(
            self.total.at[z], self.from_r.at[z], self.ls.at[z], self.rr.at[z], (2 * (self.z - 1) + self.x, self.h)
        )

    def begin(self):
        for z in self.order:
            self.to_x(z).start()

    def step(self, k):
        z = self.order[k]
        self.to_x(z).wait_recv()
        self.total[z] = (self.src[z, self.x].astype(F32) + self.from_x[z].astype(F32)).astype(BF)

        @pl.when(self.z < z)
        def _():
            @pl.when(self.z >= 1)
            def _():
                self.up(z).wait_recv()
                self.total[z] = (self.total[z].astype(F32) + self.from_l[z].astype(F32)).astype(BF)

            self.up(z).start()

        @pl.when(self.z > z)
        def _():
            @pl.when(self.z + 1 < self.nz)
            def _():
                self.down(z).wait_recv()
                self.total[z] = (self.total[z].astype(F32) + self.from_r[z].astype(F32)).astype(BF)

            self.down(z).start()

    def finish(self, result):
        for z in range(self.nz):
            self.to_x(z).wait_send()

            @pl.when(self.z < z)
            def _():
                self.up(z).wait_send()

            @pl.when(self.z > z)
            def _():
                self.down(z).wait_send()

            @pl.when(self.z == z)
            def _():
                result[...] = self.src[z, self.x].astype(F32) + self.from_x[z].astype(F32)

                @pl.when(self.z >= 1)
                def _():
                    self.up(z).wait_recv()
                    result[...] += self.from_l[z].astype(F32)

                @pl.when(self.z + 1 < self.nz)
                def _():
                    self.down(z).wait_recv()
                    result[...] += self.from_r[z].astype(F32)


class Sum:
    def __init__(self, bufs, b, h, nb):
        self.b, self.h, self.nb = b, h, nb
        self.acc, self.got, self.send, self.recv = bufs
        self.steps = Sum.step_list(nb)

    @staticmethod
    def step_list(nb):
        steps = [("h", 1), ("h", 2)]
        d = 1
        while d < nb:
            steps.append(("b", d))
            d *= 2
        return steps

    @staticmethod
    def scratch(nb, shape):
        n = len(Sum.step_list(nb))
        return [
            pltpu.VMEM((n + 1,) + shape, F32), pltpu.VMEM((n,) + shape, F32),
            pltpu.SemaphoreType.DMA((n,)), pltpu.SemaphoreType.DMA((n,)),
        ]

    def peer(self, i):
        kind, d = self.steps[i]
        return (self.b, other(self.h, d)) if kind == "h" else (other(self.b, d), self.h)

    def edges(self):
        return [(True, self.peer(i)) for i in range(len(self.steps))]

    def copy(self, i):
        return copy_to(self.acc.at[i], self.got.at[i], self.send.at[i], self.recv.at[i], self.peer(i))

    def begin(self, value):
        self.acc[0] = value
        self.copy(0).start()

    def step(self, i):
        self.copy(i).wait()
        self.acc[i + 1] = self.acc[i] + self.got[i]
        if i + 1 < len(self.steps):
            self.copy(i + 1).start()

    def result(self):
        return self.acc[len(self.steps)]


def reduce_kernel(
    nb,
    gwr_ref, gw1_ref, small_ref,
    w1all_ref, *rest,
):
    b, h = place()
    rpb = D // nb
    per = nb // NH
    share = (XC + 128) // per
    easy = share % 128 == 0
    if easy:
        ffn_ref, mix_ref, att_ref, fo_ref, small_out = rest[:5]
        rest = rest[5:]
    else:
        wr_out, small_out = rest[:2]
        rest = rest[2:]
    a, rest = rest[:10], rest[10:]
    c, rest = rest[:10], rest[10:]
    s, rest = rest[:4], rest[4:]
    res1, res2, g0, g1 = rest[:4]
    rest = rest[4:]
    line2, line1 = LineReduce(gwr_ref, a, b, h, nb), LineReduce(gw1_ref, c, b, h, nb)
    total = Sum(s, b, h, nb)
    edges = head_edges(b, h) + line_edges(b, h, nb) + total.edges()
    if easy:
        msg, got, fmsg, fgot, msend, mrecv, fsend, frecv = rest
        target = [(per * h + i, b // per) for i in range(per)]
        source = [(per * h + i, b // per) for i in range(per)]
        for i in range(per):
            away = (target[i][0] != b) | (target[i][1] != h)
            edges.append((away, target[i]))
    barrier(edges)
    line2.begin()
    line1.begin()
    total.begin(small_ref[...])
    n = len(line2.order)
    for k in range(n):
        line2.step(k)
        if k < len(total.steps):
            total.step(k)
    line2.finish(res2)
    if easy:
        for i, to in enumerate((h // 2, 2 + h // 2)):
            fmsg[i] = res2[:, i * FG : (i + 1) * FG].astype(BF)
            slot = lax.rem(h, 2)

            @pl.when(to != h)
            def _():
                copy_to(fmsg.at[i], fgot.at[slot], fsend.at[i], frecv.at[slot], (b, to)).start()

            @pl.when(to == h)
            def _():
                fgot[slot] = fmsg[i]

        for i in range(per):
            for j in range(2):
                msg[i, j] = res2[:, 2 * FG + j * FG + i * share : 2 * FG + j * FG + (i + 1) * share].astype(BF)
            bb, hh = target[i]
            slot = lax.rem(b, per)
            away = (bb != b) | (hh != h)

            @pl.when(away)
            def _():
                copy_to(msg.at[i], got.at[slot], msend.at[i], mrecv.at[slot], (bb, hh)).start()

            @pl.when(jnp.logical_not(away))
            def _():
                got[slot] = msg[i]
    else:
        wr_out[...] = res2[...]
    for k in range(n):
        line1.step(k)
        if n + k < len(total.steps):
            total.step(n + k)
    for k in range(2 * n, len(total.steps)):
        total.step(k)
    line1.finish(res1)
    w1all_ref[h] = res1[...].astype(BF)
    gather = HeadGather(lambda i: w1all_ref.at[i], b, h, (g0, g1))
    gather.begin()
    small_out[...] = total.result()
    if easy:
        for j in range(2):
            src_h = 2 * lax.rem(h, 2) + j

            @pl.when(src_h != h)
            def _():
                copy_to(fmsg.at[0], fgot.at[j], fsend.at[0], frecv.at[j], (b, src_h)).wait_recv()

            ffn_ref[:, j * FG : (j + 1) * FG] = fgot[j].astype(F32)
        for j in range(per):
            bb, hh = source[j]

            @pl.when((bb != b) | (hh != h))
            def _():
                copy_to(msg.at[0], got.at[j], msend.at[0], mrecv.at[j], (bb, hh)).wait_recv()

            out = got[j, 0].astype(F32).T
            cols = slice(j * rpb, (j + 1) * rpb)
            mix_ref[:, cols] = out[: XC // per]
            att_ref[:, cols] = out[XC // per :]
            fo_ref[:, cols] = got[j, 1].astype(F32).T
        for i, to in enumerate((h // 2, 2 + h // 2)):

            @pl.when(to != h)
            def _():
                copy_to(fmsg.at[i], fgot.at[0], fsend.at[i], frecv.at[0], (b, to)).wait_send()

        for i in range(per):
            bb, hh = target[i]

            @pl.when((bb != b) | (hh != h))
            def _():
                copy_to(msg.at[i], got.at[0], msend.at[i], mrecv.at[0], (bb, hh)).wait_send()

    gather.forward()
    gather.finish()


def reduce(nb, gwr, gw1, small):
    rpb, per = D // nb, nb // NH
    share = (XC + 128) // per
    easy = share % 128 == 0
    dma = pltpu.SemaphoreType.DMA
    outs = [vm((NH, rpb, W1C), BF)]
    if easy:
        outs += [
            vm((rpb, 2 * FG), F32), vm((XC // per, per * rpb), F32), vm((128 // per, per * rpb), F32),
            vm((FG // per, per * rpb), F32), vm(small.shape, F32),
        ]
    else:
        outs += [vm((rpb, WRC), F32), vm(small.shape, F32)]
    scratch = (
        LineReduce.scratch(nb, WRC) + LineReduce.scratch(nb, W1C) + Sum.scratch(nb, small.shape)
        + [pltpu.VMEM((rpb, W1C), F32), pltpu.VMEM((rpb, WRC), F32)] + HeadGather.scratch()
    )
    if easy:
        scratch += [
            pltpu.VMEM((per, 2, rpb, share), BF), pltpu.VMEM((per, 2, rpb, share), BF),
            pltpu.VMEM((2, rpb, FG), BF), pltpu.VMEM((2, rpb, FG), BF),
            dma((per,)), dma((per,)), dma((2,)), dma((2,)),
        ]
    shape = (nb // 2, 2, rpb)
    return call(
        functools.partial(reduce_kernel, nb), outs, scratch,
        (gwr.reshape(shape + (WRC,)), gw1.reshape(shape + (W1C,)), small), "reduce", 5,
    )


def on_device(
    inputs, cotangent, doc_starts, norm_one, mixer_in, conv_weight, conv_bias, dt_bias, a_log, d_skip, ssm_gain,
    mixer_out, attn_in, attn_out, norm_two, ffn_in, ffn_out,
):
    nb = lax.axis_size("blk")
    head = lax.axis_index("head")
    tok = inputs.shape[1]
    T = tok * NH
    longest = min(MAXLEN, T * nb // 2)
    reach = (longest + T - 2) // T
    shard = mixer_in.shape[0]
    rpb = shard * NH

    gains = jnp.stack([norm_one, norm_two], axis=1)
    mix_t, att_t, ffn_t = mixer_out.T, attn_out.T, ffn_out.T
    first, rest = [], []
    for i in range(NH):
        kv = QHEADS * HDIM + 128 * (i % 2) + HDIM * (i // 2)
        first.append(
            jnp.concatenate(
                [
                    mixer_in[:, i * XC : (i + 1) * XC],
                    mixer_in[:, DI + i * XC : DI + (i + 1) * XC],
                    mixer_in[:, 2 * DI + 128 * (i % 2) : 2 * DI + 128 * (i % 2) + 128],
                    attn_in[:, i * 128 : (i + 1) * 128],
                    attn_in[:, kv : kv + HDIM],
                    mixer_in[:, 2 * DI + 2 * STATE + i * HG : 2 * DI + 2 * STATE + (i + 1) * HG],
                    gains,
                    jnp.zeros((shard, 128 - HDIM - HG - 2), BF),
                ],
                axis=1,
            )
        )
        rest.append(
            jnp.concatenate(
                [
                    ffn_in[:, i * FG : (i + 1) * FG],
                    ffn_in[:, FF + i * FG : FF + (i + 1) * FG],
                    mix_t[:, i * XC : (i + 1) * XC],
                    att_t[:, i * 128 : (i + 1) * 128],
                    ffn_t[:, i * FG : (i + 1) * FG],
                ],
                axis=1,
            )
        )
    first, rest = jnp.stack(first), jnp.stack(rest)
    local_pieces = shard % 16 == 0
    if not local_pieces:
        first, rest = (
            lax.all_to_all(v, "head", split_axis=0, concat_axis=0, tiled=True).reshape(rpb, v.shape[2])
            for v in (first, rest)
        )
    lane = np.arange(128) % HDIM % (HDIM // 2)
    freq = jnp.asarray((10000.0 ** (-(lane.astype(np.float32) * 2.0 / HDIM))).astype(np.float32))[None, :]
    conv_b, gain = conv_bias[None, :], ssm_gain[None, :]

    (normed, gate, xin, bc, q, kv, dt, cotg, w1, wr, gain_rows, cosine, sine) = front(
        nb, inputs, cotangent, first, rest, freq, local_pieces
    )
    ylow, gated, attnf, attnl, r, lse, pre, state, kvh = mixer(
        nb, reach, xin, bc, q, kv, dt, gate, doc_starts, conv_weight, conv_b, dt_bias, a_log, d_skip, gain
    )
    result, gh, gy, ggate, gattn, gwr, gn2, ggain = feed(
        nb, gated, attnl, inputs, cotangent, cotg, wr, gain_rows, ylow, gate, r, gain
    )
    gin, gw1, gcw, gsmall, gn1 = back(
        nb, reach, gy, gattn, q, kvh, attnf, lse, pre, xin, bc, dt, state, ggate, doc_starts, conv_weight, conv_b,
        dt_bias, a_log, d_skip, cosine, sine, normed, w1, inputs, gh, gain_rows,
    )
    wide = DI + 2 * STATE
    conv = lax.dynamic_update_slice(jnp.zeros((5, DI), F32), gcw[:5, :XC], (0, head * XC))
    rows = [
        jnp.concatenate([conv, gcw[:5, XC:]], axis=1),
        lax.dynamic_update_slice(jnp.zeros((1, wide), F32), ggain, (0, head * XC)),
        jnp.pad(jnp.concatenate([gn1, gn2], axis=0), ((0, 0), (0, wide - D))),
        lax.dynamic_update_slice(jnp.zeros((8, wide), F32), gsmall[:3, :HG], (0, head * HG)),
    ]
    reduced = reduce(nb, gwr, gw1, jnp.concatenate(rows, axis=0))
    w1all, small = reduced[0].astype(F32), reduced[-1]
    part = lambda i, a, b: w1all[i, :, a:b]
    groups = range(NH)
    bc0, q0, kv0 = 2 * XC, 2 * XC + 128, 2 * XC + 256
    full_m = jnp.concatenate(
        [part(i, 0, XC) for i in groups]
        + [part(i, XC, 2 * XC) for i in groups]
        + [part(i + 2 * y, bc0 + HDIM * y, bc0 + HDIM * (y + 1)) for i in range(2) for y in range(2)]
        + [part(i, kv0 + HDIM, kv0 + HDIM + HG) for i in groups],
        axis=1,
    )
    full_a = jnp.concatenate(
        [part(i, q0, q0 + 128) for i in groups] + [part(i + 2 * y, kv0, kv0 + HDIM) for i in range(2) for y in range(2)],
        axis=1,
    )
    wide_m, wide_a = full_m.shape[1] // NH, full_a.shape[1] // NH
    g_mix_in = lax.dynamic_slice_in_dim(full_m, head * wide_m, wide_m, 1)
    g_att_in = lax.dynamic_slice_in_dim(full_a, head * wide_a, wide_a, 1)
    if len(reduced) == 6:
        g_ffn_in, g_mix_out, g_att_out, g_ffn_out = reduced[1:5]
    else:
        per = nb // NH
        blk = lax.axis_index("blk")
        mine = lax.all_gather(reduced[1][:, : 2 * FG].astype(BF), "head").reshape(NH, rpb, 2, FG)
        ffn = jnp.transpose(mine, (1, 2, 0, 3)).reshape(rpb, 2 * FF)
        g_ffn_in = lax.dynamic_slice_in_dim(ffn, head * (2 * FF // NH), 2 * FF // NH, 1).astype(F32)
        outs = lax.all_gather(reduced[1][:, 2 * FG :].astype(BF), ("blk", "head")).reshape(nb, NH, rpb, 2 * FG)
        outs = jnp.transpose(outs, (1, 3, 0, 2)).reshape(NH, 2, per, FG // per, D)
        outs = lax.dynamic_slice_in_dim(outs, head * (D // NH), D // NH, 4)
        outs = jnp.transpose(outs, (0, 2, 1, 3, 4)).reshape(nb, 2, FG // per, D // NH)
        outs = lax.dynamic_index_in_dim(outs, blk, 0, False).astype(F32)
        g_mix_out, g_att_out, g_ffn_out = outs[0, : XC // per], outs[0, XC // per :], outs[1]
    return (
        result, gin, small[6, :D], g_mix_in, small[:4], small[4], small[8, :MHEADS], small[9, :MHEADS],
        small[10, :MHEADS], small[5, :DI], g_mix_out, g_att_in, g_att_out, small[7, :D], g_ffn_in, g_ffn_out,
    )


def solution(mesh):
    both = ("blk", "head")
    tokens, rows, cols = P(None, both, None), P(both, None), P(None, both)
    split = P("blk", "head")
    return jax.shard_map(
        on_device,
        mesh=mesh,
        in_specs=(
            tokens, tokens, P(), P(both), rows, P(), P(), P(), P(), P(), P(), cols, rows, cols, P(both), rows, cols,
        ),
        out_specs=(
            tokens, tokens, P(), split, P(), P(), P(), P(), P(), P(), split, split, split, P(), split, split,
        ),
        check_vma=False,
    )
```

time: 1210 us -> 466 us (0.39)
  Pallas kernels: 0 us -> 421 us
  blocking collectives: 280 us -> 0 us
  waiting for transfers between devices: 262 us -> 0 us
  starting transfers between devices: 223 us -> 0 us
  matrix products: 132 us -> 0 us
  other arithmetic: 103 us -> 4.43 us
  local copies, waits for them, and re-layouts: 123 us -> 30.3 us
  loops' own time: 45.3 us -> 0 us
  between operations: 27.7 us -> 1.13 us
    pallas_call x0 -> x5, Pallas kernels: none -> 421 us  [call(): pl.pallas_call(kernel, out_shape=outs, in_specs=in_specs, out_specs=out_s...]
    all_gather x6 -> x0, blocking collectives: 181 us -> none  [the longest x4 109 us: prefix(): lax.all_gather(a.astype(kind), axis)]
    all_to_all x39 -> x0, waiting for transfers between devices: 139 us -> none  [the longest x2 13.7 us: micro_step(): lax.all_to_all(spread_rows(second_low), 'head', split_axis=1, concat_axis...]
    all_to_all x39 -> x0, starting transfers between devices: 139 us -> none  [the longest x2 8.71 us: micro_step(): lax.all_to_all(spread_rows(activated_low), 'head', split_axis=1, concat_a...]
    dot_general x92 -> x0, matrix products: 132 us -> none  [the longest x12 32.5 us: matmul_nt(): lax.dot_general(left_op, right_op, (((1,), (1,)), ((), ())), preferred_el...]
    ppermute x44 -> x0, starting transfers between devices: 83.2 us -> none  [shifted_2(): lax.ppermute(value, axis, [(source, source + steps) for source in range(f...]
    reduce_scatter x6 -> x0, waiting for transfers between devices: 54 us -> none  [the longest x1 54 us: on_device(): lax.psum_scatter(big_grads[1], 'blk', scatter_dimension=0, tiled=True)]
    another operation x40 -> x0, loops' own time: 45.3 us -> none  [the longest x2 16.4 us: micro_step(): lax.scan(earlier_step, (kv_heads, local_attn), step_list)]
  transfers between devices with their start and end apart: 95 -> 0, of which waited for: 48 -> 0; matrix products, arithmetic and copies ran while one was open for 27% -> 0% of each run, Pallas kernels for 0% -> 0%
where the time goes in v1:
time: 466 us; the launch traced here: 457 us
  Pallas kernels  421 us (90%)
  local copies, waits for them, and re-layouts  30.3 us (7%)
    pallas_call x5, Pallas kernels, call(): pl.pallas_call(kernel, out_shape=outs, in_specs=in_specs, out_specs=out_s...  421 us
    unnamed x34, local copies, waits for them, and re-layouts  11.4 us

profile of v1, /device:TPU:0, one launch (start us, length us, event | category | flops | bytes accessed | tf_op | source)
XLA Modules:
  0.0 457.3 jit_solution(15422946298926423398)
XLA Ops:
  0.6 0.0 copy-start.3
  0.7 0.0 copy-start.9
  0.7 0.0 copy-start.10
  0.7 0.8 constant_dynamic-update-slice_fusion.4
  1.5 0.8 constant_dynamic-update-slice_fusion.3
  2.3 0.8 constant_dynamic-update-slice_fusion.2
  3.2 0.8 constant_dynamic-update-slice_fusion.1
  3.9 0.0 copy-start.6
  3.9 0.0 copy-start.5
  4.0 0.8 constant_dynamic-update-slice_fusion
  4.8 0.9 pad_maximum_fusion.wrp_ref
  5.6 0.9 fusion.1
  6.5 0.0 copy-done.3
  6.5 0.7 fusion.2
  7.3 0.9 fusion
  8.2 0.1 fusion.4
  8.3 0.0 copy-done.9
  8.3 0.1 copy.34
  8.4 0.0 copy-done.10
  8.4 0.1 copy.35
  8.5 0.1 concatenate.43
  8.6 0.1 concatenate.44
  8.7 0.1 concatenate.45
  8.8 0.1 concatenate.46
  8.9 0.8 pad_maximum_fusion.1.w1p_ref
  9.7 103.0 %front.1 = (bf16[2,272,1024]{2,1,0:T(8,128)(2,1)}, f32[2,256,384]{2,1,0:T(8,128)}, bf16[2,272,384]{2,1,0:T(8,128)(2,1)}, bf16[2,272,256]{2,1,0:T(8,128)(2,1)}, b...) custom-call(bf16[2,64,1024]{2,1,0:T(8,128)(2,1)} %x_ref.5, ...), custom_call_target="tpu_custom_call" | custom-call | tf_op jit(solution)/shard_map/front/pallas_call | solution.py:429
  112.7 0.6 broadcast_in_dim.19.cb_ref
  113.3 0.0 copy-done.5
  113.3 0.6 broadcast_in_dim.20.gain_ref
  113.9 26.3 %mixer.1 = (bf16[2,256,384]{2,1,0:T(8,128)(2,1)}, bf16[2,256,384]{2,1,0:T(8,128)(2,1)}, f32[2,256,128]{2,1,0:T(8,128)}, bf16[2,256,128]{2,1,0:T(8,128)(2,1)}, f3...) custom-call(bf16[2,272,384]{2,1,0:T(8,128)(2,1)} %get-tuple-element., ...), custom_call_target="tpu_custom_call" | custom-call | tf_op jit(solution)/shard_map/mixer/pallas_call | solution.py:429
  140.2 54.9 %feed.1 = (f32[2,64,1024]{2,1,0:T(8,128)}, f32[2,64,1024]{2,1,0:T(8,128)}, bf16[2,256,384]{2,1,0:T(8,128)(2,1)}, bf16[2,256,384]{2,1,0:T(8,128)(2,1)}, bf16[2,25...) custom-call(bf16[2,256,384]{2,1,0:T(8,128)(2,1)} %get-tuple-element.63.gated_ref, ...), custom_call_target="tpu_custom_call" | custom-call | tf_op jit(solution)/shard_map/feed/pallas_call | solution.py:429
  195.1 85.6 %back.1 = (f32[2,64,1024]{2,1,0:T(8,128)}, bf16[1024,1152]{1,0:T(8,128)(2,1)}, f32[8,640]{1,0:T(8,128)}, f32[8,128]{1,0:T(8,128)}, f32[1,1024]{1,0:T(1,128)}) custom-call(bf16[2,256,384]{2,1,0:T(8,128)(2,1)} %get-tuple-element.71.gy_ref, bf16[2,256,128]{2,1,0:T(8,128)(2,1)} %get-tuple-element.72.gattn_ref, bf16[2,256,128]{2,1,0:T(8,128)(2,1)} %get-tuple-element.59.q_ref, ...), custom_call_target="tpu_custom_call" | custom-call | tf_op jit(solution)/shard_map/back/pallas_call | solution.py:429
  280.7 0.7 select_maximum_fusion
  281.4 0.7 slice.277
  282.1 0.3 dynamic_update_slice.11
  282.4 0.7 slice_dynamic-update-slice_fusion
  283.1 0.7 slice.276
  283.9 0.7 pad_maximum_fusion.2.small_ref
  284.5 151.7 %reduce.5 = (bf16[4,128,1152]{2,1,0:T(8,128)(2,1)}, f32[128,1024]{1,0:T(8,128)}, f32[192,256]{1,0:T(8,128)}, f32[64,256]{1,0:T(8,128)}, f32[256,256]{1,0:T(8,128)}, /*index=5*/f32[16,1792]{1,0:T(8,128)}) custom-call(bf16[4,2,128,2048]{3,2,1,0:T(8,128)(2,1)} %bitcast.71, bf16[4,2,128,1152]{3,2,1,0:T(8,128)(2,1)} %bitcast.72, ...), custom_call_target="tpu_custom_call" | custom-call | tf_op jit(solution)/shard_map/reduce/pallas_call | solution.py:429
  436.2 1.4 convert_element_type.5
  437.7 0.8 slice_bitcast_fusion.8
  438.5 0.1 concatenate.55
  438.6 0.1 constant_dynamic-slice_fusion
  438.7 0.7 copy.43
  439.4 0.9 slice_bitcast_fusion
  440.3 0.8 slice_bitcast_fusion.16
  441.1 1.4 concatenate.54
  442.5 0.0 copy-start
  442.5 0.0 copy-start.4
  442.5 0.0 copy-start.1
  442.5 0.2 constant_dynamic-slice_fusion.1
  442.7 0.9 copy.42
  443.7 1.4 slice.295
  445.1 1.4 fusion.3
  446.5 1.4 slice_reduce_fusion
  448.0 1.4 slice_reduce_fusion.1
  449.4 1.3 slice_bitcast_fusion.24
  450.7 1.9 copy.69
  452.6 0.8 copy.70
  453.4 1.6 copy.71
  455.0 0.0 copy-done.4
  455.0 0.6 copy.72
  455.6 0.8 copy.73
  456.4 0.7 copy.74
  (15 shorter events, 0.1 us)
Async XLA Ops:
  0.6 5.9 %copy-start.3 = (bf16[32,768]{1,0:T(8,128)(2,1)S(1)}, bf16[32,768]{1,0:T(8,128)(2,1)}, u32[]{:S(2)}) copy-start(bf16[32,768]{1,0:T(8,128)(2,1)} %param.30) | copy-start | bytes 147460
  0.7 7.6 %copy-start.9 = (bf16[32]{0:T(256)(128)(2,1)S(1)}, bf16[32]{0:T(256)(128)(2,1)}, u32[]{:S(2)}) copy-start(bf16[32]{0:T(256)(128)(2,1)} %param.21) | copy-start | bytes 196
  0.7 7.7 %copy-start.10 = (bf16[32]{0:T(256)(128)(2,1)S(1)}, bf16[32]{0:T(256)(128)(2,1)}, u32[]{:S(2)}) copy-start(bf16[32]{0:T(256)(128)(2,1)} %param.32) | copy-start | bytes 196
  3.9 108.7 %copy-start.6 = (f32[1792]{0:T(1024)S(1)}, f32[1792]{0:T(1024)}, u32[]{:S(2)}) copy-start(f32[1792]{0:T(1024)} %param.24) | copy-start | bytes 21508
  3.9 109.3 %copy-start.5 = (f32[1536]{0:T(1024)S(1)}, f32[1536]{0:T(1024)}, u32[]{:S(2)}) copy-start(f32[1536]{0:T(1024)} %param.28) | copy-start | bytes 18436
  195.0 85.6 %copy-start.7 = (f32[1,1024]{1,0:T(1,128)S(1)}, f32[1,1024]{1,0:T(1,128)}, u32[]{:S(2)}) copy-start(f32[1,1024]{1,0:T(1,128)} %get-tuple-element.90) | copy-start | bytes 12292
  195.1 88.8 %copy-start.8 = (f32[1,384]{1,0:T(1,128)S(1)}, f32[1,384]{1,0:T(1,128)}, u32[]{:S(2)}) copy-start(f32[1,384]{1,0:T(1,128)} %get-tuple-element.88) | copy-start | bytes 4612
  442.5 10.1 %copy-start = (f32[2,64,1024]{2,1,0:T(8,128)S(1)}, f32[2,64,1024]{2,1,0:T(8,128)}, u32[]{:S(2)}) copy-start(f32[2,64,1024]{2,1,0:T(8,128)} %get-tuple-element.206) | copy-start | bytes 1572868
  442.5 12.5 %copy-start.4 = (f32[64,256]{1,0:T(8,128)S(1)}, f32[64,256]{1,0:T(8,128)}, u32[]{:S(2)}) copy-start(f32[64,256]{1,0:T(8,128)} %get-tuple-element.217) | copy-start | bytes 196612
  442.5 13.1 %copy-start.1 = (f32[128,1024]{1,0:T(8,128)S(1)}, f32[128,1024]{1,0:T(8,128)}, u32[]{:S(2)}) copy-start(f32[128,1024]{1,0:T(8,128)} %get-tuple-element.219) | copy-start | bytes 1572868
  442.7 13.7 %copy-start.2 = (f32[256,256]{1,0:T(8,128)S(1)}, f32[256,256]{1,0:T(8,128)}, u32[]{:S(2)}) copy-start(f32[256,256]{1,0:T(8,128)} %get-tuple-element.220) | copy-start | bytes 786436
